TPU v7x, 256 devices: a whole 4x4x8 slice. The times are simulated.
256 devices in a mesh: tile: 64 (over z, y, core), frame: 4 (over x).
Axes of the slice: x: 4, y: 4, z: 8, core: 2. Of those that a mesh axis runs over, the one named last changes fastest.
Arguments:
- feats: bfloat16 [4, 16384, 256], P('frame', 'tile'), may hold values from -6 to 6
- routes: int32 [4, 64, 64], P('frame'), may hold values from 0 to 63, as said below
- interp: bfloat16 [4, 64, 16384, 128], P('frame', None, 'tile'), may hold values from -0.5 to 0.5
- w_value: bfloat16 [256, 256], replicated, may hold values from -0.375 to 0.375
- w_attn: bfloat16 [256, 64], replicated, may hold values from -48 to 48
- w_out: bfloat16 [256, 256], replicated, may hold values from -0.375 to 0.375
- grad_out: bfloat16 [4, 16384, 256], P('frame', 'tile'), may hold values from -6 to 6
Outputs:
- grad_feats: bfloat16 [4, 16384, 256], P('frame', 'tile')
- grad_w_value: float32 [256, 256], replicated
- grad_w_attn: float32 [256, 64], replicated
- grad_w_out: float32 [256, 256], replicated
Inputs may be any that keep to these rules, and one draw needn't show every extreme that they name: `routes`: within one frame a reader tile names any one owner tile in at most 2 of its 64 columns; in every frame some owner tile is named in exactly 2 columns by every reader tile.
All inputs are finite; a program needn't handle non-finite values.
Results may differ from a plain program's by a relative error of at most 0.022.
Values may be sent and summed in bfloat16 or wider, within the bound.
A program may use at most 128 MiB of HBM per device.

v0:
```python
import math

import jax
import jax.numpy as jnp
from jax import lax
from jax.sharding import PartitionSpec as P

H = 8
L = 2
P_SIZE = 4


def per_device(feats, routes, interp, w_value, w_attn, w_out, grad_out):
    inputs_now = feats[0]
    grads_now = grad_out[0]
    tile_weights = interp[0]
    routes_now = routes[0]
    tile_count = lax.axis_size("tile")
    myself = lax.axis_index("tile")
    row_count = inputs_now.shape[0]
    model_width = inputs_now.shape[1]
    column_count = tile_weights.shape[0]
    cell_count = tile_weights.shape[2]
    head_count = H
    level_count = L
    point_count = P_SIZE
    group_width = level_count * point_count
    head_dim = model_width // head_count
    capacity = max(2, 2 * column_count // tile_count)
    column = jnp.arange(column_count, dtype=jnp.int32)
    head_of = column // group_width
    level_of = column // point_count % level_count
    lookup_index = level_of * head_count + head_of
    my_routes = lax.dynamic_index_in_dim(routes_now, myself, 0, keepdims=False)
    earlier = (my_routes[None, :] == my_routes[:, None]) & (column[None, :] < column[:, None])
    ranking = jnp.sum(earlier.astype(jnp.int32), axis=1)
    slot_index = my_routes * capacity + ranking
    aimed = routes_now == myself
    ordering = jnp.cumsum(aimed.astype(jnp.int32), axis=1) - 1
    slot_range = jnp.arange(capacity, dtype=jnp.int32)
    picked = aimed[:, None, :] & (ordering[:, None, :] == slot_range[None, :, None])
    filled = jnp.any(picked, axis=2)
    chosen = jnp.sum(jnp.where(picked, lookup_index[None, None, :], 0), axis=2)
    values = jnp.dot(inputs_now, w_value, preferred_element_type=jnp.float32).astype(jnp.bfloat16)
    lookup = values.reshape(level_count, cell_count, head_count, head_dim).transpose(0, 2, 3, 1)
    lookup = lookup.reshape(level_count * head_count, head_dim, cell_count)
    empty = jnp.zeros((column_count, head_dim, cell_count), jnp.bfloat16)
    pieces = lax.all_gather(lookup[None], "tile", axis=0, tiled=True)
    owner_count = pieces.shape[0]
    inside = (my_routes >= 0) & (my_routes < owner_count)
    found = pieces[jnp.clip(my_routes, 0, owner_count - 1), lookup_index]
    fetched = jnp.where(inside[:, None, None], found, empty)
    sampled = jnp.einsum("jdc,jqc->jdq", fetched, tile_weights, preferred_element_type=jnp.float32)
    logits = jnp.dot(inputs_now, w_attn, preferred_element_type=jnp.float32)
    attn = jax.nn.softmax(logits.reshape(row_count, head_count, group_width), axis=-1).reshape(
        row_count, column_count
    )
    attn_heads = attn.T.reshape(head_count, group_width, 1, row_count)
    sampled_heads = sampled.reshape(head_count, group_width, head_dim, row_count)
    mixed = (
        jnp.sum(attn_heads * sampled_heads, axis=1)
        .reshape(model_width, row_count)
        .T.astype(jnp.bfloat16)
    )
    grad_mixed = jnp.dot(grads_now, w_out.T, preferred_element_type=jnp.float32)
    grad_mixed_heads = grad_mixed.T.reshape(head_count, 1, head_dim, row_count)
    grad_attn = jnp.sum(grad_mixed_heads * sampled_heads, axis=2).reshape(column_count, row_count).T
    grad_attn = grad_attn.reshape(row_count, head_count, group_width)
    attn_query = attn.reshape(row_count, head_count, group_width)
    inner_term = jnp.sum(attn_query * grad_attn, axis=-1, keepdims=True)
    grad_logits = (
        (attn_query * (grad_attn - inner_term))
        .reshape(row_count, column_count)
        .astype(jnp.bfloat16)
    )
    grad_sampled = (
        (attn_heads * grad_mixed_heads)
        .reshape(column_count, head_dim, row_count)
        .astype(jnp.bfloat16)
    )
    contrib = jnp.einsum(
        "jdq,jqc->jdc", grad_sampled, tile_weights, preferred_element_type=jnp.float32
    )
    outgoing = (
        jnp.zeros((tile_count * capacity, head_dim, cell_count), jnp.float32)
        .at[slot_index]
        .set(contrib)
    )
    returned = lax.all_to_all(
        outgoing.reshape(tile_count, capacity, head_dim, cell_count).astype(jnp.bfloat16),
        "tile",
        split_axis=0,
        concat_axis=0,
        tiled=True,
    ).astype(jnp.float32)
    table_range = jnp.arange(level_count * head_count, dtype=jnp.int32)
    member = (chosen.reshape(-1)[None, :] == table_range[:, None]) & filled.reshape(-1)[None, :]
    grad_lookup = jnp.dot(
        member.astype(jnp.float32),
        returned.reshape(tile_count * capacity, head_dim * cell_count),
        precision=lax.Precision.HIGHEST,
    )
    grad_values = grad_lookup.reshape(level_count, head_count, head_dim, cell_count).transpose(
        0, 3, 1, 2
    )
    grad_values = grad_values.reshape(row_count, model_width).astype(jnp.bfloat16)
    grad_query = jnp.dot(grad_logits, w_attn.T, preferred_element_type=jnp.float32)
    part_attn = jnp.dot(inputs_now.T, grad_logits, preferred_element_type=jnp.float32)
    part_out = jnp.dot(mixed.T, grads_now, preferred_element_type=jnp.float32)
    grad_inputs = grad_query + jnp.dot(grad_values, w_value.T, preferred_element_type=jnp.float32)
    part_value = jnp.dot(inputs_now.T, grad_values, preferred_element_type=jnp.float32)
    totals = lax.psum((part_value, part_attn, part_out), ("tile", "frame"))
    factor = 1.0 / math.sqrt(tile_count * lax.axis_size("frame") * row_count)
    return (
        grad_inputs.astype(jnp.bfloat16)[None],
        totals[0] * factor,
        totals[1] * factor,
        totals[2] * factor,
    )


def solution(mesh):
    in_specs = (
        P("frame", "tile", None),
        P("frame", None, None),
        P("frame", None, "tile", None),
        P(),
        P(),
        P(),
        P("frame", "tile", None),
    )
    out_specs = (P("frame", "tile", None), P(), P(), P())
    return jax.shard_map(
        per_device, mesh=mesh, in_specs=in_specs, out_specs=out_specs, check_vma=False
    )
```

profile of v0, /device:TPU:1, one launch (start us, length us, event | category | flops | bytes accessed | tf_op | source)
XLA Modules:
  0.0 408.1 jit_solution(1071865935539580949)
XLA Ops:
  7.2 0.0 copy-start
  7.2 0.0 all-gather.2.cloned.1.call-start
  7.2 0.8 copy-done
  8.1 1.1 convolution_convert_fusion
  9.2 0.1 copy.28
  9.3 0.7 copy.29
  10.0 0.0 all-gather.2.cloned.1.call-update
  10.0 0.7 compare_and_fusion
  10.7 0.2 convert_reduce_fusion
  10.9 1.0 fusion.13
  11.9 1.2 fusion.25
  13.1 85.5 %all-gather.2.cloned.1.call-done = bf16[64,16,32,128]{3,2,1,0:T(8,128)(2,1)} async-done(((bf16[1,16,32,128]{3,2,1,0:T(8,128)(2,1)}), bf16[64,16,32,128]{3,2,1,0:T(8,128)(2,1)}) %all-gather.2.cloned.1.call-update) | async-done | bytes 8388624 | tf_op jit(solution)/shard_map/all_gather | solution.py:48
  98.7 4.1 %gather_fusion = bf16[64,32,128]{2,1,0:T(8,128)(2,1)S(1)} fusion(bf16[64,16,32,128]{3,2,1,0:T(8,128)(2,1)} %all-gather.2.cloned.1.call-done, s32[64]{0:T(128)S(1)} %get-tuple-element.30), kind=kCustom, calls=%fused_computation | custom fusion | bytes 1049088 | tf_op jit(solution)/shard_map/gather | solution.py:51
  102.8 5.2 %fusion.8 = (bf16[64,32,256]{2,1,0:T(8,128)(2,1)S(1)}, f32[64,256]{1,0:T(8,128)S(1)}, f32[64,32,256]{2,1,0:T(8,128)}) fusion(f32[64,256]{1,0:T(8,128)S(1)} %bitcast.145, f32[8,32,256]{2,1,0:T(8,128)S(1)} %fusion.25, bf16[1,64,256,128]{3,2,1,0:T(8,128)(2,1)} %param.9, bf16[64,32,128]{2,1,0:T(8,128)(2,1)S(1)} %gather_fusion, ...), kind=kOutput, calls=%fused_computation.12 | convolution fusion | flops 136560640 | bytes 8257600 | tf_op jit(solution)/shard_map/jdc,jqc->jdq/dot_general | solution.py:53
  108.0 0.7 fusion.3
  108.7 0.3 broadcast_in_dim.30
  109.0 2.5 scatter_fusion
  111.5 0.0 copy-start.5
  111.5 1.2 convert_element_type.58
  112.7 6.4 %all-to-all-start = ((bf16[64,2,32,128]{3,2,1,0:T(8,128)(2,1)}), bf16[64,2,32,128]{3,2,1,0:T(8,128)(2,1)S(1)}, u32[]{:S(2)}, u32[]{:S(2)}) async-start(bf16[64,2,32,128]{3,2,1,0:T(8,128)(2,1)} %bitcast.26), calls=%async_computation | async-start | bytes 2097152 | tf_op jit(solution)/shard_map/all_to_all | solution.py:89
  119.1 0.0 all-reduce.3.cloned.1.call-start
  119.1 0.0 copy-done.5
  119.2 0.2 reduce_window_sum.11
  119.4 0.1 select_reduce_fusion
  119.5 0.1 copy.30
  119.6 0.1 eq.77
  119.8 0.1 fusion.45
  119.9 0.1 copy.31
  120.0 0.2 and.128
  120.2 0.3 multiply_reduce_fusion
  120.5 0.8 convolution_bitcast_fusion.1
  121.3 1.8 fusion.27
  123.1 24.0 %all-to-all-done = bf16[64,2,32,128]{3,2,1,0:T(8,128)(2,1)S(1)} async-done(((bf16[64,2,32,128]{3,2,1,0:T(8,128)(2,1)}), bf16[64,2,32,128]{3,2,1,0:T(8,128)(2,1)S(1)}, u32[]{:S(2)}, u32[]{:S(2)}) %all-to-all-start) | async-done | bytes 1048608 | tf_op jit(solution)/shard_map/all_to_all | solution.py:89
  147.1 0.5 copy.50
  147.5 0.0 copy-start.6
  147.5 0.0 copy-start.3
  147.5 0.7 copy.32
  148.2 0.4 fusion.11
  148.6 0.2 copy.33
  148.8 0.9 convolution_bitcast_fusion
  149.7 0.0 all-reduce.3.cloned.1.call-update
  149.7 0.2 fusion.19
  150.0 0.9 fusion.10
  150.8 247.0 %all-reduce.3.cloned.1.call-done = (f32[256,256]{0,1:T(8,128)}, f32[256,64]{0,1:T(8,128)}, f32[256,256]{0,1:T(8,128)}) async-done(((f32[256,256]{0,1:T(8,128)}, f32[256,64]{0,1:T(8,128)}, f32[256,256]{0,1:T(8,128)}), (f32[256,256]{0,1:T(8,128)}, f32[256,64]{0,1:T(8,128)}, f32[256,256]{0,1:T(8,128)})) %all-reduce.3.cloned.1.call-update) | async-done | bytes 589840 | tf_op jit(solution)/shard_map/psum | solution.py:112
  397.8 1.1 broadcast_multiply_fusion
  398.9 0.8 copy.35
  399.8 0.8 copy.36
  400.6 0.6 broadcast_multiply_fusion.2
  (14 shorter events, 0.1 us)
Async XLA Ops:
  7.2 0.9 copy-start
  7.2 91.5 %all-gather.2.cloned.1.call-start = ((), (), s32[]{:S(2)}) async-start(), calls=%async_computation.1 | async-start | bytes 8519680 | tf_op jit(solution)/shard_map/all_gather | solution.py:48
  102.8 5.3 %copy-start.1 = (bf16[1,64,256,128]{3,2,1,0:T(8,128)(2,1)S(1)}, bf16[1,64,256,128]{3,2,1,0:T(8,128)(2,1)}, u32[]{:S(2)}) copy-start(bf16[1,64,256,128]{3,2,1,0:T(8,128)(2,1)} %param.9) | copy-start | bytes 12582916
  111.5 7.6 %copy-start.5 = (s32[1,64,64]{2,1,0:T(8,128)S(1)}, s32[1,64,64]{2,1,0:T(8,128)}, u32[]{:S(2)}) copy-start(s32[1,64,64]{2,1,0:T(8,128)} %param.8) | copy-start | bytes 49156
  112.7 7.5 %copy-start.2 = (f32[64,32,256]{2,1,0:T(8,128)S(1)}, f32[64,32,256]{2,1,0:T(8,128)}, u32[]{:S(2)}) copy-start(f32[64,32,256]{2,1,0:T(8,128)} %get-tuple-element.31) | copy-start | bytes 6291460
  112.7 34.4 %all-to-all-start = ((bf16[64,2,32,128]{3,2,1,0:T(8,128)(2,1)}), bf16[64,2,32,128]{3,2,1,0:T(8,128)(2,1)S(1)}, u32[]{:S(2)}, u32[]{:S(2)}) async-start(bf16[64,2,32,128]{3,2,1,0:T(8,128)(2,1)} %bitcast.26), calls=%async_computation | async-start | bytes 2097152 | tf_op jit(solution)/shard_map/all_to_all | solution.py:89
  119.1 278.7 %all-reduce.3.cloned.1.call-start = ((), (), s32[]{:S(2)}) async-start(), calls=%async_computation.2 | async-start | bytes 1179648 | tf_op jit(solution)/shard_map/psum | solution.py:112
  147.5 2.2 copy-start.6
  147.5 2.4 copy-start.3
  397.8 2.8 copy-start.4
Sparse Core Ops, SparseCore 0:
  11.4 87.2 all-gather.1
  149.8 247.9 all-reduce.2
where the time goes:
time: 408 us
  waiting for transfers between devices  357 us (88%)
  between operations  14.3 us (4%)
  matrix products  14.2 us (3%)
  local copies, waits for them, and re-layouts  12 us (3%)
  starting transfers between devices  6.44 us (2%)
  other arithmetic  4.6 us (1%)
    psum x1, waiting for transfers between devices, per_device(): totals = lax.psum((part_value, part_attn, part_out), ('tile', 'frame'))  247 us
    all_gather x1, waiting for transfers between devices, per_device(): pieces = lax.all_gather(lookup[None], 'tile', axis=0, tiled=True)  85.5 us
    all_to_all x1, waiting for transfers between devices, per_device(): lax.all_to_all(outgoing.reshape(tile_count, capacity, head_dim, cell_coun...  24 us
  transfers between devices with their start and end apart: 3, of which 3 were waited for; matrix products, arithmetic and copies ran while one was open for 2% of the time, Pallas kernels for 0%

commit v1 on v0

v1 whole, which is shorter than its diff:
```python
import math

import jax
import jax.numpy as jnp
from jax import lax
from jax.experimental import pallas as pl
from jax.experimental.pallas import tpu as pltpu
from jax.sharding import PartitionSpec as P

MESH = pl.DeviceIdType.MESH
F32 = jnp.float32
BF16 = jnp.bfloat16
NZ = 8
NP = 8
NX = 4
H = 8
HALF = 2048
SHARE = 144
NN = (((1,), (0,)), ((), ()))
NT = (((1,), (1,)), ((), ()))


def dot(a, b, dims=NN):
    return lax.dot_general(a, b, dims, preferred_element_type=F32)


def block(index, size):
    return pl.ds(pl.multiple_of(index * size, size), size)


def kernel(
    feats, routes, interp, w_value, w_attn_t, w_out, grad_out,
    grad_feats, grad_w_value, grad_w_attn_t, grad_w_out,
    itp, v_rows, ag, send_f, recv_f, send_r, recv_r, acc,
    rs_send, rs_recv, con, con_rows, fet, attn_s, gm_s, ga_s, mixed_s, feats_t,
    pick_f, pick_r, mine_t, mine, route_s, gv_rows,
    rp_send, rp_recv, share_s, rz_send, rz_recv, rx_recv, gz, gp,
    itp_sem, bar_unused, ag_send_sem, ag_recv_sem, f_send_sem, f_recv_sem,
    r_send_sem, r_recv_sem, rs_send_sem, rs_recv_sem,
    p_send_sem, p_recv_sem, z_send_sem, z_recv_sem, x_send_sem, x_recv_sem,
    gz_send_sem, gz_recv_sem, gp_send_sem, gp_recv_sem,
):
    t = lax.axis_index("tile")
    f = lax.axis_index("frame")
    z = lax.div(t, NP)
    p = lax.rem(t, NP)

    def plane_tile(i):
        return z * NP + lax.rem(p + i, NP)

    def column_tile(i):
        return lax.rem(z + i, NZ) * NP + p

    right = column_tile(1)
    left = column_tile(NZ - 1)

    def remote(src, dst, send_sem, recv_sem, tile, frame):
        return pltpu.make_async_remote_copy(
            src_ref=src, dst_ref=dst, send_sem=send_sem, recv_sem=recv_sem,
            device_id=(tile, frame), device_id_type=MESH,
        )

    loads = [
        pltpu.make_async_copy(
            interp.at[0, pl.ds(h * 8, 8)], itp.at[pl.ds(h * 8, 8)], itp_sem.at[h]
        )
        for h in range(H)
    ]
    for load in loads:
        load.start()

    barrier = pltpu.get_barrier_semaphore()
    for i in range(1, NP):
        pl.semaphore_signal(barrier, inc=1, device_id=(plane_tile(i), f), device_id_type=MESH)
    for i in range(1, NZ):
        pl.semaphore_signal(barrier, inc=1, device_id=(column_tile(i), f), device_id_type=MESH)
    for i in range(1, NX):
        pl.semaphore_signal(barrier, inc=1, device_id=(t, lax.rem(f + i, NX)), device_id_type=MESH)

    values = dot(feats[0], w_value[...])
    values_t = values.T
    v_rows[0:256] = values_t[:, 0:128]
    v_rows[256:512] = values_t[:, 128:256]
    for half in range(2):
        def spread(e, _, half=half):
            d = half * 16 + e
            tiles = [v_rows[pl.ds(l * 256 + d, 8, stride=32), :] for l in range(2)]
            ag[half, 0:16, block(e, 128)] = jnp.concatenate(tiles, axis=0).astype(BF16)
            return 0
        lax.fori_loop(0, 16, spread, 0)

    pl.semaphore_wait(barrier, NP - 1 + NZ - 1 + NX - 1)

    def ring(side, s, half):
        if side == 0:
            src, dst, to = (NZ - s) % NZ, NZ - 1 - s, right
        else:
            src, dst, to = s, s + 1, left
        return remote(
            ag.at[half, pl.ds(src * 16, 16)], ag.at[half, pl.ds(dst * 16, 16)],
            ag_send_sem.at[side, s, half], ag_recv_sem.at[side, s, half], to, f,
        )

    ring_steps = [
        [(side, s, half) for half in range(2) for side in range(2) if s < 3 or half == side]
        for s in range(4)
    ]
    for step in ring_steps[0]:
        ring(*step).start()

    route_s[...] = jnp.full(route_s.shape, -1, jnp.int32)
    route_s[:, 0:64] = routes[0, block(z, NP), :]
    row = lax.broadcasted_iota(jnp.int32, (128, 128), 0)
    lane = lax.broadcasted_iota(jnp.int32, (128, 128), 1)
    row_rel = lax.rem(lax.div(row, 2), 8)
    row_slot = lax.rem(row, 2)
    row_plane = lax.div(row, 16)
    owner_z = lax.rem(z + row_rel, NZ) * NP

    def picks(named, owner):
        hit = named == owner
        first = jnp.min(jnp.where(hit, lane, 128), axis=1, keepdims=True)
        is_first = jnp.where(lane == first, 1, 0)
        return jnp.where(hit & (is_first == 1 - row_slot), 1.0, 0.0).astype(F32)

    mine_now = picks(jnp.broadcast_to(route_s[pl.ds(p, 1), :], (128, 128)), owner_z + row_plane)
    mine_t[...] = mine_now.astype(BF16)
    mine[...] = mine_now.T.astype(BF16)
    readers = jnp.broadcast_to(route_s[...][:, None, :], (8, 16, 128)).reshape(128, 128)
    asked = picks(readers, owner_z + p)
    piece_of = lax.rem(lax.div(row, 4), 2) * 8 + lax.div(row, 8)
    pieces = jnp.where(piece_of == lax.rem(lane, 16), 1.0, 0.0).astype(BF16)
    to_piece = dot(asked.astype(BF16), pieces)
    to_piece = jnp.where(row_rel == lax.div(lane, 16), to_piece, 0.0)
    pick_f[...] = to_piece.astype(BF16)
    pick_r[...] = to_piece.T.astype(BF16)

    logits = dot(w_attn_t[...], feats[0], NT).reshape(H, 8, 256)
    powers = jnp.exp(logits - jnp.max(logits, axis=1, keepdims=True))
    attn_s[...] = (powers / jnp.sum(powers, axis=1, keepdims=True)).reshape(64, 256)
    gm_s[...] = dot(w_out[...], grad_out[0], NT)
    feats_t[...] = feats[0].astype(F32).T.astype(BF16)

    for h in range(H):
        loads[h].wait()

    def contribute(h, _):
        grad_mixed = gm_s[block(h, 32), :]
        weights = attn_s[block(h, 8), :]
        for i in range(8):
            grad_sampled = (weights[i:i + 1] * grad_mixed).astype(BF16)
            con[block(h * 8 + i, 32), :] = dot(grad_sampled, itp[h * 8 + i])
        return 0
    lax.fori_loop(0, H, contribute, 0)

    def plane_copy(send, recv, send_sem, recv_sem, half, i):
        return remote(
            send.at[half, block(lax.rem(p + i, NP), 16)], recv.at[half, block(p, 16)],
            send_sem.at[half, i - 1], recv_sem.at[half, i - 1], plane_tile(i), f,
        )

    def plane_wait(recv, recv_sem, half, i):
        there = recv.at[half, block(lax.rem(p + NP - i, NP), 16)]
        pltpu.make_async_copy(there, there, recv_sem.at[half, i - 1]).wait()

    for half in range(2):
        def lay(e, _, half=half):
            d = half * 16 + e
            for g in range(4):
                tiles = [con[pl.ds((g * 2 + k) * 256 + d, 8, stride=32), :] for k in range(2)]
                con_rows[half, g * 16:(g + 1) * 16, block(e, 128)] = jnp.concatenate(tiles, axis=0).astype(BF16)
            return 0
        lax.fori_loop(0, 16, lay, 0)

        def choose(e, _, half=half):
            send_r[half, :, block(e, 512)] = dot(
                mine_t[:, 0:64], con_rows[half, :, block(e, 512)]
            ).astype(BF16)
            return 0
        lax.fori_loop(0, 4, choose, 0)
        for i in range(1, NP):
            plane_copy(send_r, recv_r, r_send_sem, r_recv_sem, half, i).start()
        recv_r[half, block(p, 16), :] = send_r[half, block(p, 16), :]

    for s in range(1, 4):
        for side, _, half in ring_steps[s - 1]:
            ring(side, s - 1, half).wait_recv()
            if (side, s, half) in ring_steps[s]:
                ring(side, s, half).start()
    for step in ring_steps[3]:
        ring(*step).wait_recv()

    for half in range(2):
        def answer(e, _, half=half):
            send_f[half, :, block(e, 512)] = dot(pick_f[...], ag[half, :, block(e, 512)]).astype(BF16)
            return 0
        lax.fori_loop(0, 4, answer, 0)
        for i in range(1, NP):
            plane_copy(send_f, recv_f, f_send_sem, f_recv_sem, half, i).start()
        recv_f[half, block(p, 16), :] = send_f[half, block(p, 16), :]

    def chain(side, s, half):
        return remote(
            rs_send.at[side, s, half], rs_recv.at[side, s, half],
            rs_send_sem.at[side, s, half], rs_recv_sem.at[side, s, half],
            right if side == 0 else left, f,
        )

    def chain_send(side, s, half):
        rel = 4 - s if side == 0 else 4 + s
        total = acc[half, rel * 16:(rel + 1) * 16, :]
        if s >= 1 and (side, s - 1, half) in chain_steps[s - 1]:
            chain(side, s - 1, half).wait_recv()
            total = total + rs_recv[side, s - 1, half].astype(F32)
        rs_send[side, s, half] = total.astype(BF16)
        chain(side, s, half).start()

    chain_steps = [
        [(side, s, half) for half in range(2) for side in range(2) if s > 0 or half == side]
        for s in range(4)
    ]
    for half in range(2):
        for i in range(1, NP):
            plane_wait(recv_r, r_recv_sem, half, i)
        def add_up(e, _, half=half):
            acc[half, :, block(e, 512)] = dot(pick_r[...], recv_r[half, :, block(e, 512)])
            return 0
        lax.fori_loop(0, 4, add_up, 0)
        chain_send(half, 0, half)
    for s in range(1, 4):
        for step in chain_steps[s]:
            chain_send(*step)

    for half in range(2):
        for i in range(1, NP):
            plane_wait(recv_f, f_recv_sem, half, i)
        def fetch(e, _, half=half):
            rows = dot(mine[0:64, :], recv_f[half, :, block(e, 512)])
            for k in range(4):
                d = half * 16 + e * 4 + k
                for g in range(8):
                    fet[pl.ds(g * 256 + d, 8, stride=32), :] = rows[g * 8:(g + 1) * 8, k * 128:(k + 1) * 128]
            return 0
        lax.fori_loop(0, 4, fetch, 0)

    def sample(h, _):
        grad_mixed = gm_s[block(h, 32), :]
        weights = attn_s[block(h, 8), :]
        mixed = jnp.zeros((32, 256), F32)
        grads = []
        for i in range(8):
            j = h * 8 + i
            sampled = dot(fet[block(j, 32), :].astype(BF16), itp[j], NT)
            mixed = mixed + weights[i:i + 1] * sampled
            grads.append(jnp.sum(grad_mixed * sampled, axis=0, keepdims=True))
        mixed_s[block(h, 32), :] = mixed.astype(BF16)
        ga_s[block(h, 8), :] = jnp.concatenate(grads, axis=0)
        return 0
    lax.fori_loop(0, H, sample, 0)

    attn = attn_s[...].reshape(H, 8, 256)
    grad_attn = ga_s[...].reshape(H, 8, 256)
    inner = jnp.sum(attn * grad_attn, axis=1, keepdims=True)
    grad_logits = (attn * (grad_attn - inner)).reshape(64, 256)
    part_attn = dot(grad_logits.astype(BF16), feats[0])
    part_out = dot(mixed_s[...], grad_out[0])
    grad_query = dot(grad_logits.T.astype(BF16), w_attn_t[...])

    for half in range(2):
        total = acc[half, 0:16, :]
        for side in range(2):
            chain(side, 3, half).wait_recv()
            total = total + rs_recv[side, 3, half].astype(F32)
        for e in range(16):
            for l in range(2):
                gv_rows[pl.ds(l * 256 + half * 16 + e, 8, stride=32), :] = total[l * 8:(l + 1) * 8, e * 128:(e + 1) * 128]
    grad_values = jnp.concatenate([gv_rows[0:256].T, gv_rows[256:512].T], axis=0).astype(BF16)
    part_value = dot(feats_t[...], grad_values)

    for q in range(NP):
        lanes = slice((q // 4) * 128, (q // 4 + 1) * 128)
        k = q % 4
        rp_send[q, 0:64] = part_value[k * 64:(k + 1) * 64, lanes].astype(BF16)
        rp_send[q, 64:128] = part_out[k * 64:(k + 1) * 64, lanes].astype(BF16)
        rp_send[q, 128:144] = part_attn[k * 16:(k + 1) * 16, lanes].astype(BF16)

    def share_copy(i):
        return remote(
            rp_send.at[lax.rem(p + i, NP)], rp_recv.at[i - 1],
            p_send_sem.at[i - 1], p_recv_sem.at[i - 1], plane_tile(i), f,
        )
    for i in range(1, NP):
        share_copy(i).start()
    grad_feats[0] = (grad_query + dot(grad_values, w_value[...], NT)).astype(BF16)
    total = rp_send[p].astype(F32)
    for i in range(1, NP):
        share_copy(i).wait_recv()
        total = total + rp_recv[i - 1].astype(F32)
    for q in range(NZ):
        rz_send[q, 0:8] = total[q * 8:(q + 1) * 8]
        rz_send[q, 8:16] = total[64 + q * 8:64 + (q + 1) * 8]
        rz_send[q, 16:32] = total[128:144]

    def column_copy(i):
        return remote(
            rz_send.at[lax.rem(z + i, NZ)], rz_recv.at[z],
            z_send_sem.at[i - 1], z_recv_sem.at[i - 1], column_tile(i), f,
        )
    for i in range(1, NZ):
        column_copy(i).start()
    rz_recv[z] = rz_send[z]
    for i in range(1, NZ):
        there = rz_recv.at[lax.rem(z + NZ - i, NZ)]
        pltpu.make_async_copy(there, there, z_recv_sem.at[i - 1]).wait()
    total = rz_recv[0]
    for q in range(1, NZ):
        total = total + rz_recv[q]
    rx_recv[f] = total

    def frame_copy(i):
        return remote(
            rx_recv.at[f], rx_recv.at[f],
            x_send_sem.at[i - 1], x_recv_sem.at[i - 1], t, lax.rem(f + i, NX),
        )
    for i in range(1, NX):
        frame_copy(i).start()
    for i in range(1, NX):
        there = rx_recv.at[lax.rem(f + NX - i, NX)]
        pltpu.make_async_copy(there, there, x_recv_sem.at[i - 1]).wait()
    total = rx_recv[0]
    for q in range(1, NX):
        total = total + rx_recv[q]
    gz[z] = total[0:16]

    def gather_column(i):
        return remote(
            gz.at[z], gz.at[z],
            gz_send_sem.at[i - 1], gz_recv_sem.at[i - 1], column_tile(i), f,
        )
    for i in range(1, NZ):
        gather_column(i).start()
    for i in range(1, NZ):
        there = gz.at[lax.rem(z + NZ - i, NZ)]
        pltpu.make_async_copy(there, there, gz_recv_sem.at[i - 1]).wait()
    gathered = [gz[q] for q in range(NZ)]
    gp[p] = jnp.concatenate(
        [g[0:8] for g in gathered] + [g[8:16] for g in gathered] + [total[16:32]], axis=0
    ).astype(BF16)

    def gather_plane(i):
        return remote(
            gp.at[p], gp.at[p],
            gp_send_sem.at[i - 1], gp_recv_sem.at[i - 1], plane_tile(i), f,
        )
    for i in range(1, NP):
        gather_plane(i).start()
    for i in range(1, NP):
        there = gp.at[lax.rem(p + NP - i, NP)]
        pltpu.make_async_copy(there, there, gp_recv_sem.at[i - 1]).wait()
    factor = 1.0 / math.sqrt(NX * NZ * NP * 256)
    for q in range(NP):
        lanes = slice((q // 4) * 128, (q // 4 + 1) * 128)
        k = q % 4
        grad_w_value[k * 64:(k + 1) * 64, lanes] = gp[q, 0:64].astype(F32) * factor
        grad_w_out[k * 64:(k + 1) * 64, lanes] = gp[q, 64:128].astype(F32) * factor
        grad_w_attn_t[k * 16:(k + 1) * 16, lanes] = gp[q, 128:144].astype(F32) * factor

    for steps in ring_steps:
        for step in steps:
            ring(*step).wait_send()
    for steps in chain_steps:
        for step in steps:
            chain(*step).wait_send()
    for half in range(2):
        for i in range(1, NP):
            plane_copy(send_f, recv_f, f_send_sem, f_recv_sem, half, i).wait_send()
            plane_copy(send_r, recv_r, r_send_sem, r_recv_sem, half, i).wait_send()
    for i in range(1, NP):
        share_copy(i).wait_send()
        gather_plane(i).wait_send()
    for i in range(1, NZ):
        column_copy(i).wait_send()
        gather_column(i).wait_send()
    for i in range(1, NX):
        frame_copy(i).wait_send()


def per_device(feats, routes, interp, w_value, w_attn, w_out, grad_out):
    vmem = pl.BlockSpec(memory_space=pltpu.VMEM)
    dma = pltpu.SemaphoreType.DMA
    outs = pl.pallas_call(
        kernel,
        out_shape=(
            jax.ShapeDtypeStruct((1, 256, 256), BF16),
            jax.ShapeDtypeStruct((256, 256), F32),
            jax.ShapeDtypeStruct((64, 256), F32),
            jax.ShapeDtypeStruct((256, 256), F32),
        ),
        in_specs=[vmem, vmem, pl.BlockSpec(memory_space=pl.ANY)] + [vmem] * 4,
        out_specs=(vmem,) * 4,
        scratch_shapes=[
            pltpu.VMEM((64, 256, 128), BF16),
            pltpu.VMEM((512, 128), F32),
            pltpu.VMEM((2, 128, HALF), BF16),
            pltpu.VMEM((2, 128, HALF), BF16),
            pltpu.VMEM((2, 128, HALF), BF16),
            pltpu.VMEM((2, 128, HALF), BF16),
            pltpu.VMEM((2, 128, HALF), BF16),
            pltpu.VMEM((2, 128, HALF), F32),
            pltpu.VMEM((2, 4, 2, 16, HALF), BF16),
            pltpu.VMEM((2, 4, 2, 16, HALF), BF16),
            pltpu.VMEM((2048, 128), F32),
            pltpu.VMEM((2, 64, HALF), BF16),
            pltpu.VMEM((2048, 128), F32),
            pltpu.VMEM((64, 256), F32),
            pltpu.VMEM((256, 256), F32),
            pltpu.VMEM((64, 256), F32),
            pltpu.VMEM((256, 256), BF16),
            pltpu.VMEM((256, 256), BF16),
            pltpu.VMEM((128, 128), BF16),
            pltpu.VMEM((128, 128), BF16),
            pltpu.VMEM((128, 128), BF16),
            pltpu.VMEM((128, 128), BF16),
            pltpu.VMEM((8, 128), jnp.int32),
            pltpu.VMEM((512, 128), F32),
            pltpu.VMEM((NP, SHARE, 128), BF16),
            pltpu.VMEM((NP - 1, SHARE, 128), BF16),
            pltpu.VMEM((SHARE, 128), F32),
            pltpu.VMEM((NZ, 32, 128), F32),
            pltpu.VMEM((NZ, 32, 128), F32),
            pltpu.VMEM((NX, 32, 128), F32),
            pltpu.VMEM((NZ, 16, 128), F32),
            pltpu.VMEM((NP, SHARE, 128), BF16),
            dma((H,)),
            pltpu.SemaphoreType.REGULAR,
            dma((2, 4, 2)),
            dma((2, 4, 2)),
            dma((2, NP - 1)),
            dma((2, NP - 1)),
            dma((2, NP - 1)),
            dma((2, NP - 1)),
            dma((2, 4, 2)),
            dma((2, 4, 2)),
            dma((NP - 1,)),
            dma((NP - 1,)),
            dma((NZ - 1,)),
            dma((NZ - 1,)),
            dma((NX - 1,)),
            dma((NX - 1,)),
            dma((NZ - 1,)),
            dma((NZ - 1,)),
            dma((NP - 1,)),
            dma((NP - 1,)),
        ],
        compiler_params=pltpu.CompilerParams(
            collective_id=0, has_side_effects=True, vmem_limit_bytes=48 * 1024 * 1024
        ),
    )(feats, routes, interp, w_value, w_attn.T, w_out, grad_out)
    return outs[0], outs[1], outs[2].T, outs[3]


def solution(mesh):
    in_specs = (
        P("frame", "tile", None),
        P("frame", None, None),
        P("frame", None, "tile", None),
        P(),
        P(),
        P(),
        P("frame", "tile", None),
    )
    out_specs = (P("frame", "tile", None), P(), P(), P())
    return jax.shard_map(
        per_device, mesh=mesh, in_specs=in_specs, out_specs=out_specs, check_vma=False
    )
```

time: 408 us -> 85.9 us (0.21)
  waiting for transfers between devices: 357 us -> 0 us
  Pallas kernels: 0 us -> 74.9 us
  matrix products: 14.2 us -> 0 us
  between operations: 14.3 us -> 0.66 us
  starting transfers between devices: 6.44 us -> 0 us
  other arithmetic: 4.6 us -> 0 us
    psum x1 -> x0, waiting for transfers between devices: 247 us -> none  [per_device(): totals = lax.psum((part_value, part_attn, part_out), ('tile', 'frame'))]
    all_gather x1 -> x0, waiting for transfers between devices: 85.5 us -> none  [per_device(): pieces = lax.all_gather(lookup[None], 'tile', axis=0, tiled=True)]
    pallas_call x0 -> x1, Pallas kernels: none -> 74.9 us  [per_device(): pl.pallas_call(kernel, out_shape=(jax.ShapeDtypeStruct((1, 256, 256), BF1...]
    all_to_all x1 -> x0, waiting for transfers between devices: 24 us -> none  [per_device(): lax.all_to_all(outgoing.reshape(tile_count, capacity, head_dim, cell_coun...]
    dot_general x10 -> x0, matrix products: 13.2 us -> none  [the longest x1 5.25 us: per_device(): jnp.einsum('jdc,jqc->jdq', fetched, tile_weights, preferred_element_type=...]
    unnamed x17 -> x18, local copies, waits for them, and re-layouts: 3.01 us -> 10 us
    all_to_all x1 -> x0, starting transfers between devices: 6.36 us -> none  [per_device(): lax.all_to_all(outgoing.reshape(tile_count, capacity, head_dim, cell_coun...]
    gather x1 -> x0, local copies, waits for them, and re-layouts: 4.12 us -> none  [per_device(): found = pieces[jnp.clip(my_routes, 0, owner_count - 1), lookup_index]]
  transfers between devices with their start and end apart: 3 -> 0, of which waited for: 3 -> 0; matrix products, arithmetic and copies ran while one was open for 2% -> 0% of each run, Pallas kernels for 0% -> 0%
where the time goes in v1:
time: 85.9 us; the launch traced here: 85.5 us
  Pallas kernels  74.9 us (87%)
  local copies, waits for them, and re-layouts  10 us (12%)
    pallas_call x1, Pallas kernels, per_device(): pl.pallas_call(kernel, out_shape=(jax.ShapeDtypeStruct((1, 256, 256), BF1...  74.9 us
    unnamed x18, local copies, waits for them, and re-layouts  10 us

profile of v1, /device:TPU:1, one launch (start us, length us, event | category | flops | bytes accessed | tf_op | source)
XLA Modules:
  0.0 85.5 jit_solution(16677151421184209569)
XLA Ops:
  0.6 0.0 copy-start
  0.6 2.2 %copy-done = bf16[1,64,256,128]{3,2,1,0:T(8,128)(2,1)S(1)} copy-done((bf16[1,64,256,128]{3,2,1,0:T(8,128)(2,1)S(1)}, bf16[1,64,256,128]{3,2,1,0:T(8,128)(2,1)}, u32[]{:S(2)}) %copy-start) | copy-done | bytes 4194328
  2.8 0.0 copy-start.1
  2.8 0.9 %copy-done.1 = bf16[1,256,256]{2,1,0:T(8,128)(2,1)S(1)} copy-done((bf16[1,256,256]{2,1,0:T(8,128)(2,1)S(1)}, bf16[1,256,256]{2,1,0:T(8,128)(2,1)}, u32[]{:S(2)}) %copy-start.1) | copy-done | bytes 131096
  3.7 0.0 copy-start.2
  3.7 0.9 %copy-done.2 = bf16[256,256]{1,0:T(8,128)(2,1)S(1)} copy-done((bf16[256,256]{1,0:T(8,128)(2,1)S(1)}, bf16[256,256]{1,0:T(8,128)(2,1)}, u32[]{:S(2)}) %copy-start.2) | copy-done | bytes 131096
  4.6 0.0 copy-start.3
  4.6 0.9 %copy-done.3 = bf16[256,256]{1,0:T(8,128)(2,1)S(1)} copy-done((bf16[256,256]{1,0:T(8,128)(2,1)S(1)}, bf16[256,256]{1,0:T(8,128)(2,1)}, u32[]{:S(2)}) %copy-start.3) | copy-done | bytes 131096
  5.5 0.0 copy-start.4
  5.5 0.9 %copy-done.4 = bf16[1,256,256]{2,1,0:T(8,128)(2,1)S(1)} copy-done((bf16[1,256,256]{2,1,0:T(8,128)(2,1)S(1)}, bf16[1,256,256]{2,1,0:T(8,128)(2,1)}, u32[]{:S(2)}) %copy-start.4) | copy-done | bytes 131096
  6.4 0.0 copy-start.5
  6.4 0.8 copy-done.5
  7.2 0.0 copy-start.6
  7.2 0.8 copy-done.6
  8.0 74.9 %shard_map.102 = (bf16[1,256,256]{2,1,0:T(8,128)(2,1)S(1)}, f32[256,256]{1,0:T(8,128)S(1)}, f32[64,256]{1,0:T(8,128)S(1)}, f32[256,256]{1,0:T(8,128)S(1)}) custom-call(bf16[1,256,256]{2,1,0:T(8,128)(2,1)S(1)} %copy-done.1, s32[1,64,64]{2,1,0:T(8,128)S(1)} %copy-done.5, bf16[1,64,256,128]{3,2,1,0:T(8,128)(2,1)S(1)} %copy-done, ...), custom_call_target="tpu_custom_call" | custom-call | tf_op jit(solution)/shard_map/pallas_call | solution.py:391
  82.8 0.7 copy.15
  83.5 0.7 copy.16
  84.2 0.6 copy.17
  84.8 0.7 copy.18
Async XLA Ops:
  0.6 2.2 %copy-start = (bf16[1,64,256,128]{3,2,1,0:T(8,128)(2,1)S(1)}, bf16[1,64,256,128]{3,2,1,0:T(8,128)(2,1)}, u32[]{:S(2)}) copy-start(bf16[1,64,256,128]{3,2,1,0:T(8,128)(2,1)} %interp.1) | copy-start | bytes 12582916
  2.8 0.9 %copy-start.1 = (bf16[1,256,256]{2,1,0:T(8,128)(2,1)S(1)}, bf16[1,256,256]{2,1,0:T(8,128)(2,1)}, u32[]{:S(2)}) copy-start(bf16[1,256,256]{2,1,0:T(8,128)(2,1)} %feats.1) | copy-start | bytes 393220
  3.7 0.9 %copy-start.2 = (bf16[256,256]{1,0:T(8,128)(2,1)S(1)}, bf16[256,256]{1,0:T(8,128)(2,1)}, u32[]{:S(2)}) copy-start(bf16[256,256]{1,0:T(8,128)(2,1)} %w_value.1) | copy-start | bytes 393220
  4.6 0.9 %copy-start.3 = (bf16[256,256]{1,0:T(8,128)(2,1)S(1)}, bf16[256,256]{1,0:T(8,128)(2,1)}, u32[]{:S(2)}) copy-start(bf16[256,256]{1,0:T(8,128)(2,1)} %w_out.1) | copy-start | bytes 393220
  5.5 0.9 %copy-start.4 = (bf16[1,256,256]{2,1,0:T(8,128)(2,1)S(1)}, bf16[1,256,256]{2,1,0:T(8,128)(2,1)}, u32[]{:S(2)}) copy-start(bf16[1,256,256]{2,1,0:T(8,128)(2,1)} %grad_out.1) | copy-start | bytes 393220
  6.4 0.8 copy-start.5
  7.2 0.8 copy-start.6

commit v2 on v0

v2 whole, which is shorter than its diff:
```python
import math

import jax
import jax.numpy as jnp
from jax import lax
from jax.experimental import pallas as pl
from jax.experimental.pallas import tpu as pltpu
from jax.sharding import PartitionSpec as P

MESH = pl.DeviceIdType.MESH
F32 = jnp.float32
BF16 = jnp.bfloat16
NZ = 8
NP = 8
NX = 4
H = 8
SHARE = 144
PLACE = {0: 0, 1: 1, 7: 2, 2: 3, 6: 4, 3: 5, 5: 6, 4: 7}
GROUPS = ((0, 1), (1, 2), (3, 2), (5, 2), (7, 1))
NN = (((1,), (0,)), ((), ()))
NT = (((1,), (1,)), ((), ()))


def dot(a, b, dims=NN):
    return lax.dot_general(a, b, dims, preferred_element_type=F32)


def block(index, size):
    return pl.ds(pl.multiple_of(index * size, size), size)


def one_hot(hit):
    return jnp.where(hit, 1.0, 0.0).astype(BF16)


def kernel(
    feats_hbm, routes_hbm, interp, w_value_hbm, w_attn_hbm, w_out_hbm, grad_out_hbm,
    grad_feats, sums,
    feats, routes, w_value, w_attn_t, w_out, grad_out, itp, v_rows,
    ag, send_f, recv_f, send_r, recv_r, acc, rs_send, rs_recv,
    con, con_rows, fet, fetched, attn_s, gm_s, ga_s, mixed_s, feats_t,
    pick_f, pick_r, mine_t, mine, route_s, gv_rows,
    rp_send, rp_recv, rz_send, rz_recv, rx_recv, gz, gp,
    in_sem, itp_sem, ag_send_sem, ag_recv_sem, f_send_sem, f_recv_sem,
    r_send_sem, r_recv_sem, rs_send_sem, rs_recv_sem, sum_send_sem, sum_recv_sem,
):
    t = lax.axis_index("tile")
    f = lax.axis_index("frame")
    z = lax.div(t, NP)
    p = lax.rem(t, NP)

    def plane_tile(i):
        return z * NP + lax.rem(p + i, NP)

    def column_tile(i):
        return lax.rem(z + i, NZ) * NP + p

    right = column_tile(1)
    left = column_tile(NZ - 1)

    leaving, coming = [], {}

    def remote(src, dst, send_sem, recv_sem, tile, frame):
        return pltpu.make_async_remote_copy(
            src_ref=src, dst_ref=dst, send_sem=send_sem, recv_sem=recv_sem,
            device_id=(tile, frame), device_id_type=MESH,
        )

    def send(key, copy):
        copy.start()
        leaving.append(copy.wait_send)
        coming[key] = copy.wait_recv

    def send_many(key, copies, size, send_sem, recv_sem):
        for copy in copies:
            copy.start()
        leaving.append(pltpu.make_async_copy(size, size, send_sem).wait)
        coming[key] = pltpu.make_async_copy(size, size, recv_sem).wait

    def arrive(key):
        coming.pop(key)()

    def settle():
        for key in list(coming):
            arrive(key)
        for wait in leaving:
            wait()

    barrier = pltpu.get_barrier_semaphore()
    near = [(plane_tile(i), f) for i in range(1, NP)] + [(right, f), (left, f)]
    near += [(t, lax.rem(f + i, NX)) for i in range(1, NX)]
    for device in near:
        pl.semaphore_signal(barrier, inc=1, device_id=device, device_id_type=MESH)

    ins = [
        pltpu.make_async_copy(src, dst, in_sem.at[i])
        for i, (src, dst) in enumerate((
            (feats_hbm, feats), (w_value_hbm, w_value), (routes_hbm, routes),
            (w_attn_hbm, w_attn_t), (w_out_hbm, w_out), (grad_out_hbm, grad_out),
        ))
    ]
    loads = [
        pltpu.make_async_copy(
            interp.at[0, pl.ds(h * 8, 8)], itp.at[pl.ds(h * 8, 8)], itp_sem.at[h]
        )
        for h in range(H)
    ]
    for load in ins + loads:
        load.start()

    ins[0].wait()
    ins[1].wait()
    values_t = dot(feats[0], w_value[...]).T
    v_rows[0:256] = values_t[:, 0:128]
    v_rows[256:512] = values_t[:, 128:256]
    for k in range(0, 16, 2):
        for c in range(4):
            tiles = [v_rows[pl.ds((k + m) * 32 + c, 8, stride=4), :] for m in range(2)]
            ag[0, k * 8:(k + 2) * 8, c * 128:(c + 1) * 128] = jnp.concatenate(tiles, axis=0).astype(BF16)
    for load in ins[2:]:
        load.wait()

    route_s[...] = jnp.full(route_s.shape, -1, jnp.int32)
    route_s[:, 0:64] = routes[0, block(z, NP), :]
    row = lax.broadcasted_iota(jnp.int32, (128, 128), 0)
    lane = lax.broadcasted_iota(jnp.int32, (128, 128), 1)
    place = lax.div(row, 16)
    distance = jnp.where(lax.rem(place, 2) == 1, lax.div(place + 1, 2), NZ - lax.div(place, 2))
    row_slot = lax.rem(row, 2)
    row_plane = lax.rem(lax.div(row, 2), NP)
    owner_z = lax.rem(z + distance, NZ) * NP

    def picks(named, owner):
        hit = named == owner
        first = jnp.min(jnp.where(hit, lane, 128), axis=1, keepdims=True)
        is_first = jnp.where(lane == first, 1, 0)
        return jnp.where(hit & (is_first == 1 - row_slot), 1.0, 0.0).astype(F32)

    def same_row(shape):
        return lax.rem(lax.broadcasted_iota(jnp.int32, shape, 0), 8) == lax.rem(
            lax.broadcasted_iota(jnp.int32, shape, 1), 8
        )

    def by_eight(x):
        return jnp.broadcast_to(x[:, None, :], (x.shape[0], 8, x.shape[1])).reshape(x.shape[0] * 8, x.shape[1])

    def eighth(shape):
        return one_hot(
            lax.div(lax.broadcasted_iota(jnp.int32, shape, 1), 8) == lax.broadcasted_iota(jnp.int32, shape, 0)
        )

    mine_now = picks(jnp.broadcast_to(route_s[pl.ds(p, 1), :], (128, 128)), owner_z + row_plane)
    mine_wide = dot(mine_now.astype(BF16), eighth((128, 512)))
    mine_wide_t = dot(mine_now.T[0:64].astype(BF16), eighth((128, 1024)))
    readers = jnp.broadcast_to(
        jnp.broadcast_to(route_s[...][:, None, :], (8, 2, 128)).reshape(16, 128)[None], (8, 16, 128)
    ).reshape(128, 128)
    asked = picks(readers, owner_z + p)
    piece_of = lax.rem(lax.div(row, 4), 2) * 8 + lax.div(row, 8)
    to_piece = dot(asked.astype(BF16), one_hot(piece_of == lax.div(lane, 8)))
    keep = same_row((128, 128))
    keep_wide = same_row((128, 512))
    keep_long = same_row((512, 128))
    for q in range(8):
        mine_t[q] = jnp.where(keep_wide, by_eight(mine_wide[q * 16:(q + 1) * 16]), 0.0).astype(BF16)
        mine[:, q * 128:(q + 1) * 128] = jnp.where(
            keep_long, by_eight(mine_wide_t[:, q * 128:(q + 1) * 128]), 0.0
        ).astype(BF16)
        piece = jnp.where(keep, by_eight(to_piece[q * 16:(q + 1) * 16]), 0.0)
        pick_f[q] = piece.astype(BF16)
        pick_r[q] = piece.T.astype(BF16)

    logits = dot(w_attn_t[...], feats[0], NT).reshape(H, 8, 256)
    powers = jnp.exp(logits - jnp.max(logits, axis=1, keepdims=True))
    attn_s[...] = (powers / jnp.sum(powers, axis=1, keepdims=True)).reshape(64, 256)
    gm_s[...] = dot(w_out[...], grad_out[0], NT)

    for load in loads:
        load.wait()

    def contribute(h, _):
        grad_mixed = gm_s[block(h, 32), :]
        weights = attn_s[block(h, 8), :]
        for i in range(8):
            grad_sampled = (weights[i:i + 1] * grad_mixed).astype(BF16)
            con[i * 32:(i + 1) * 32, :] = dot(grad_sampled, itp[h * 8 + i])
        for i in range(0, 8, 2):
            for c in range(4):
                tiles = [con[pl.ds((i + m) * 32 + c, 8, stride=4), :] for m in range(2)]
                con_rows[block(h * 4 + i // 2, 16), c * 128:(c + 1) * 128] = jnp.concatenate(tiles, axis=0).astype(BF16)
        return 0
    lax.fori_loop(0, H, contribute, 0)

    def choose(q, _):
        send_r[q] = dot(mine_t[q], con_rows[...]).astype(BF16)
        return 0
    lax.fori_loop(0, 8, choose, 0)

    def answer(q):
        send_f[q] = dot(pick_f[q], ag[q]).astype(BF16)
    answer(0)

    pl.semaphore_wait(barrier, len(near))

    def ring(side, s, half):
        if side == 0:
            src, dst, to = (NZ - s) % NZ, NZ - 1 - s, right
        else:
            src, dst, to = s, s + 1, left
        rows = pl.ds(half * 64, 64)
        return remote(
            ag.at[PLACE[src], rows], ag.at[PLACE[dst], rows],
            ag_send_sem.at[side, s, half], ag_recv_sem.at[side, s, half], to, f,
        )

    ring_steps = [
        [(side, s, half) for order in range(2) for side in range(2)
         for half in ((side + order) % 2,) if s < 3 or half == side]
        for s in range(4)
    ]
    for step in ring_steps[0]:
        send(("ring", *step), ring(*step))

    def plane_send(name, src, dst, send_sem, recv_sem, g):
        first, count = GROUPS[g]
        blocks = pl.ds(first, count)
        copies = [
            remote(
                src.at[blocks, block(lax.rem(p + i, NP), 16)], dst.at[blocks, block(p, 16)],
                send_sem.at[g], recv_sem.at[g], plane_tile(i), f,
            )
            for i in range(1, NP)
        ]
        send_many((name, g), copies, dst.at[blocks, pl.ds(0, 16 * (NP - 1))], send_sem.at[g], recv_sem.at[g])
        for q in range(first, first + count):
            dst[q, block(p, 16), :] = src[q, block(p, 16), :]

    for g in (4, 3, 2, 1, 0):
        plane_send("r", send_r, recv_r, r_send_sem, r_recv_sem, g)
    plane_send("f", send_f, recv_f, f_send_sem, f_recv_sem, 0)
    feats_t[...] = feats[0].astype(F32).T.astype(BF16)

    def chain(side, s, half):
        rows = pl.ds(half * 64, 64)
        return remote(
            rs_send.at[side, s, rows], rs_recv.at[side, s, rows],
            rs_send_sem.at[side, s, half], rs_recv_sem.at[side, s, half],
            right if side == 0 else left, f,
        )

    def add_up(g):
        arrive(("r", g))
        for q in range(GROUPS[g][0], GROUPS[g][0] + GROUPS[g][1]):
            acc[q] = dot(pick_r[q], recv_r[q])

    def chain_send(side, s, half):
        rows = slice(half * 64, half * 64 + 64)
        total = acc[PLACE[4 - s if side == 0 else 4 + s], rows]
        if s > 1 or (s == 1 and half == side):
            arrive(("chain", side, s - 1, half))
            total = total + rs_recv[side, s - 1, rows].astype(F32)
        rs_send[side, s, rows] = total.astype(BF16)
        send(("chain", side, s, half), chain(side, s, half))

    add_up(4)
    for side in range(2):
        chain_send(side, 0, side)
    for s in range(1, 4):
        for side, _, half in ring_steps[s - 1]:
            arrive(("ring", side, s - 1, half))
            if (side, s, half) in ring_steps[s]:
                send(("ring", side, s, half), ring(side, s, half))
        for q in range(GROUPS[s][0], GROUPS[s][0] + 2):
            answer(q)
        plane_send("f", send_f, recv_f, f_send_sem, f_recv_sem, s)
        add_up(4 - s)
        for order in range(2):
            for side in range(2):
                chain_send(side, s, (1 - side + order) % 2)
    for step in ring_steps[3]:
        arrive(("ring", *step))
    answer(7)
    plane_send("f", send_f, recv_f, f_send_sem, f_recv_sem, 4)
    add_up(0)

    total = acc[0]
    for side in range(2):
        for half in range(2):
            arrive(("chain", side, 3, half))
        total = total + rs_recv[side, 3].astype(F32)
    for k in range(16):
        for c in range(4):
            gv_rows[pl.ds(k * 32 + c, 8, stride=4), :] = total[k * 8:(k + 1) * 8, c * 128:(c + 1) * 128]
    grad_values = jnp.concatenate([gv_rows[0:256].T, gv_rows[256:512].T], axis=0).astype(BF16)
    part_value = dot(feats_t[...], grad_values)
    gm_value = dot(grad_values, w_value[...], NT)

    for g in range(4):
        arrive(("f", g))
    near_rows = recv_f[0:7].reshape(7 * 128, 512)

    def fetch(e, _):
        fetched[block(e, 128), :] = dot(mine[block(e, 128), 0:896], near_rows)
        return 0
    lax.fori_loop(0, 4, fetch, 0)
    arrive(("f", 4))

    def sample(h, _):
        grad_mixed = gm_s[block(h, 32), :]
        weights = attn_s[block(h, 8), :]
        maps = fetched[block(h, 64), :] + dot(mine[block(h, 64), 896:1024], recv_f[7])
        for i in range(8):
            for c in range(4):
                fet[pl.ds(i * 32 + c, 8, stride=4), :] = maps[i * 8:(i + 1) * 8, c * 128:(c + 1) * 128]
        mixed = jnp.zeros((32, 256), F32)
        grads = []
        for i in range(8):
            sampled = dot(fet[i * 32:(i + 1) * 32, :].astype(BF16), itp[h * 8 + i], NT)
            mixed = mixed + weights[i:i + 1] * sampled
            grads.append(jnp.sum(grad_mixed * sampled, axis=0, keepdims=True))
        mixed_s[block(h, 32), :] = mixed.astype(BF16)
        ga_s[block(h, 8), :] = jnp.concatenate(grads, axis=0)
        return 0
    lax.fori_loop(0, H, sample, 0)

    attn = attn_s[...].reshape(H, 8, 256)
    grad_attn = ga_s[...].reshape(H, 8, 256)
    inner = jnp.sum(attn * grad_attn, axis=1, keepdims=True)
    grad_logits = (attn * (grad_attn - inner)).reshape(64, 256)
    part_attn = dot(grad_logits.astype(BF16), feats[0])
    part_out = dot(mixed_s[...], grad_out[0])

    for q in range(NP):
        lanes = slice((q // 4) * 128, (q // 4 + 1) * 128)
        k = q % 4
        rp_send[q, 0:64] = part_value[k * 64:(k + 1) * 64, lanes].astype(BF16)
        rp_send[q, 64:128] = part_out[k * 64:(k + 1) * 64, lanes].astype(BF16)
        rp_send[q, 128:144] = part_attn[k * 16:(k + 1) * 16, lanes].astype(BF16)

    def exchange(stage, count, src, dst, device):
        send_sem, recv_sem = sum_send_sem.at[stage], sum_recv_sem.at[stage]
        copies = [remote(src(i), dst[1], send_sem, recv_sem, *device(i)) for i in range(1, count)]
        send_many(stage, copies, dst[0].at[pl.ds(0, count - 1)], send_sem, recv_sem)

    exchange(
        0, NP, lambda i: rp_send.at[lax.rem(p + i, NP)], (rp_recv, rp_recv.at[p]), lambda i: (plane_tile(i), f)
    )
    rp_recv[p] = rp_send[p]
    grad_query = dot(grad_logits.T.astype(BF16), w_attn_t[...])
    grad_feats[0] = (grad_query + gm_value).astype(BF16)
    arrive(0)
    total = rp_recv[0].astype(F32)
    for q in range(1, NP):
        total = total + rp_recv[q].astype(F32)
    for q in range(NZ):
        rows = [total[q * 8:(q + 1) * 8], total[64 + q * 8:64 + (q + 1) * 8], total[128:144]]
        rz_send[q] = jnp.concatenate(rows, axis=0).astype(BF16)
    exchange(
        1, NZ, lambda i: rz_send.at[lax.rem(z + i, NZ)], (rz_recv, rz_recv.at[z]), lambda i: (column_tile(i), f)
    )
    rz_recv[z] = rz_send[z]
    arrive(1)
    total = rz_recv[0].astype(F32)
    for q in range(1, NZ):
        total = total + rz_recv[q].astype(F32)
    rx_recv[f] = total.astype(BF16)
    exchange(
        2, NX, lambda i: rx_recv.at[f], (rx_recv, rx_recv.at[f]), lambda i: (t, lax.rem(f + i, NX))
    )
    arrive(2)
    total = rx_recv[0].astype(F32)
    for q in range(1, NX):
        total = total + rx_recv[q].astype(F32)
    gz[z] = total[0:16].astype(BF16)
    exchange(3, NZ, lambda i: gz.at[z], (gz, gz.at[z]), lambda i: (column_tile(i), f))
    arrive(3)
    gathered = [gz[q].astype(F32) for q in range(NZ)]
    gp[p] = jnp.concatenate(
        [g[0:8] for g in gathered] + [g[8:16] for g in gathered] + [total[16:32]], axis=0
    ).astype(BF16)
    exchange(4, NP, lambda i: gp.at[p], (gp, gp.at[p]), lambda i: (plane_tile(i), f))
    arrive(4)
    sums[...] = gp[...]

    settle()


def finish(grad_in, sums, grad_feats, grad_w_value, grad_w_attn_t, grad_w_out):
    factor = 1.0 / math.sqrt(NX * NZ * NP * 256)
    grad_feats[...] = grad_in[...]
    for q in range(NP):
        lanes = slice((q // 4) * 128, (q // 4 + 1) * 128)
        k = q % 4
        grad_w_value[k * 64:(k + 1) * 64, lanes] = sums[q, 0:64].astype(F32) * factor
        grad_w_out[k * 64:(k + 1) * 64, lanes] = sums[q, 64:128].astype(F32) * factor
        grad_w_attn_t[k * 16:(k + 1) * 16, lanes] = sums[q, 128:144].astype(F32) * factor


def per_device(feats, routes, interp, w_value, w_attn, w_out, grad_out):
    vmem = pl.BlockSpec(memory_space=pltpu.VMEM)
    dma = pltpu.SemaphoreType.DMA
    moved, sums = pl.pallas_call(
        kernel,
        out_shape=(
            jax.ShapeDtypeStruct((1, 256, 256), BF16),
            jax.ShapeDtypeStruct((NP, SHARE, 128), BF16),
        ),
        in_specs=[pl.BlockSpec(memory_space=pltpu.HBM)] * 7,
        out_specs=(vmem,) * 2,
        scratch_shapes=[
            pltpu.VMEM((1, 256, 256), BF16),
            pltpu.VMEM((1, 64, 64), jnp.int32),
            pltpu.VMEM((256, 256), BF16),
            pltpu.VMEM((64, 256), BF16),
            pltpu.VMEM((256, 256), BF16),
            pltpu.VMEM((1, 256, 256), BF16),
            pltpu.VMEM((64, 256, 128), BF16),
            pltpu.VMEM((512, 128), F32),
            pltpu.VMEM((8, 128, 512), BF16),
            pltpu.VMEM((8, 128, 512), BF16),
            pltpu.VMEM((8, 128, 512), BF16),
            pltpu.VMEM((8, 128, 512), BF16),
            pltpu.VMEM((8, 128, 512), BF16),
            pltpu.VMEM((8, 128, 512), F32),
            pltpu.VMEM((2, 4, 128, 512), BF16),
            pltpu.VMEM((2, 4, 128, 512), BF16),
            pltpu.VMEM((256, 128), F32),
            pltpu.VMEM((512, 512), BF16),
            pltpu.VMEM((256, 128), F32),
            pltpu.VMEM((512, 512), F32),
            pltpu.VMEM((64, 256), F32),
            pltpu.VMEM((256, 256), F32),
            pltpu.VMEM((64, 256), F32),
            pltpu.VMEM((256, 256), BF16),
            pltpu.VMEM((256, 256), BF16),
            pltpu.VMEM((8, 128, 128), BF16),
            pltpu.VMEM((8, 128, 128), BF16),
            pltpu.VMEM((8, 128, 512), BF16),
            pltpu.VMEM((512, 1024), BF16),
            pltpu.VMEM((8, 128), jnp.int32),
            pltpu.VMEM((512, 128), F32),
            pltpu.VMEM((NP, SHARE, 128), BF16),
            pltpu.VMEM((NP, SHARE, 128), BF16),
            pltpu.VMEM((NZ, 32, 128), BF16),
            pltpu.VMEM((NZ, 32, 128), BF16),
            pltpu.VMEM((NX, 32, 128), BF16),
            pltpu.VMEM((NZ, 16, 128), BF16),
            pltpu.VMEM((NP, SHARE, 128), BF16),
            dma((6,)),
            dma((H,)),
            dma((2, 4, 2)),
            dma((2, 4, 2)),
            dma((5,)),
            dma((5,)),
            dma((5,)),
            dma((5,)),
            dma((2, 4, 2)),
            dma((2, 4, 2)),
            dma((5,)),
            dma((5,)),
        ],
        compiler_params=pltpu.CompilerParams(
            collective_id=0, has_side_effects=True, vmem_limit_bytes=63 * 1024 * 1024
        ),
    )(feats, routes, interp, w_value, w_attn.T, w_out, grad_out)
    grads = pl.pallas_call(
        finish,
        out_shape=(
            jax.ShapeDtypeStruct((1, 256, 256), BF16),
            jax.ShapeDtypeStruct((256, 256), F32),
            jax.ShapeDtypeStruct((64, 256), F32),
            jax.ShapeDtypeStruct((256, 256), F32),
        ),
        in_specs=[vmem] * 2,
        out_specs=(vmem,) * 4,
    )(moved, sums)
    return grads[0], grads[1], grads[2].T, grads[3]


def solution(mesh):
    in_specs = (
        P("frame", "tile", None),
        P("frame", None, None),
        P("frame", None, "tile", None),
        P(),
        P(),
        P(),
        P("frame", "tile", None),
    )
    out_specs = (P("frame", "tile", None), P(), P(), P())
    return jax.shard_map(
        per_device, mesh=mesh, in_specs=in_specs, out_specs=out_specs, check_vma=False
    )
```

time: 408 us -> 72.6 us (0.18)
  waiting for transfers between devices: 357 us -> 0 us
  Pallas kernels: 0 us -> 71.9 us
  matrix products: 14.2 us -> 0 us
  between operations: 14.3 us -> 0.64 us
  local copies, waits for them, and re-layouts: 12 us -> 0 us
  starting transfers between devices: 6.44 us -> 0 us
  other arithmetic: 4.6 us -> 0 us
    psum x1 -> x0, waiting for transfers between devices: 247 us -> none  [per_device(): totals = lax.psum((part_value, part_attn, part_out), ('tile', 'frame'))]
    all_gather x1 -> x0, waiting for transfers between devices: 85.5 us -> none  [per_device(): pieces = lax.all_gather(lookup[None], 'tile', axis=0, tiled=True)]
    pallas_call x0 -> x2, Pallas kernels: none -> 71.9 us  [the longest x1 70 us: per_device(): pl.pallas_call(kernel, out_shape=(jax.ShapeDtypeStruct((1, 256, 256), BF1...]
    all_to_all x1 -> x0, waiting for transfers between devices: 24 us -> none  [per_device(): lax.all_to_all(outgoing.reshape(tile_count, capacity, head_dim, cell_coun...]
    dot_general x10 -> x0, matrix products: 13.2 us -> none  [the longest x1 5.25 us: per_device(): jnp.einsum('jdc,jqc->jdq', fetched, tile_weights, preferred_element_type=...]
    all_to_all x1 -> x0, starting transfers between devices: 6.36 us -> none  [per_device(): lax.all_to_all(outgoing.reshape(tile_count, capacity, head_dim, cell_coun...]
    gather x1 -> x0, local copies, waits for them, and re-layouts: 4.12 us -> none  [per_device(): found = pieces[jnp.clip(my_routes, 0, owner_count - 1), lookup_index]]
  transfers between devices with their start and end apart: 3 -> 0, of which waited for: 3 -> 0; matrix products, arithmetic and copies ran while one was open for 2% -> 0% of each run, Pallas kernels for 0% -> 0%
where the time goes in v2:
time: 72.6 us; the launch traced here: 72.5 us
  Pallas kernels  71.9 us (99%)
    pallas_call x1, Pallas kernels, per_device(): pl.pallas_call(kernel, out_shape=(jax.ShapeDtypeStruct((1, 256, 256), BF1...  70 us
    pallas_call x1, Pallas kernels, per_device(): pl.pallas_call(finish, out_shape=(jax.ShapeDtypeStruct((1, 256, 256), BF1...  1.91 us

profile of v2, /device:TPU:1, one launch (start us, length us, event | category | flops | bytes accessed | tf_op | source)
XLA Modules:
  0.0 72.5 jit_solution(3370129061846255960)
XLA Ops:
  0.6 70.0 %shard_map.102 = (bf16[1,256,256]{2,1,0:T(8,128)(2,1)}, bf16[8,144,128]{2,1,0:T(8,128)(2,1)}) custom-call(bf16[1,256,256]{2,1,0:T(8,128)(2,1)} %feats_hbm.1, s32[1,64,64]{2,1,0:T(8,128)} %routes_hbm.1, bf16[1,64,256,128]{3,2,1,0:T(8,128)(2,1)} %interp.1, bf16[256,256]{1,0:T(8,128)(2,1)} %w_value_hbm.1, bf16[64,256]{1,0:T(8,128)(2,1)} %bitcast.2, ...), custom_call_target="tpu_custom_call" | custom-call | tf_op jit(solution)/shard_map/pallas_call | solution.py:402
  70.6 1.9 %shard_map.103 = (bf16[1,256,256]{2,1,0:T(8,128)(2,1)}, f32[256,256]{1,0:T(8,128)}, f32[64,256]{1,0:T(8,128)}, f32[256,256]{1,0:T(8,128)}) custom-call(bf16[1,256,256]{2,1,0:T(8,128)(2,1)} %get-tuple-element.10.grad_in, bf16[8,144,128]{2,1,0:T(8,128)(2,1)} %get-tuple-element.11.sums), custom_call_target="tpu_custom_call" | custom-call | tf_op jit(solution)/shard_map/pallas_call | solution.py:466

commit v3 on v2

--- a/solution.py
+++ b/solution.py
@@ -14,7 +14,7 @@
 NP = 8
 NX = 4
 H = 8
-SHARE = 144
+SHARES = (64, 80)
 PLACE = {0: 0, 1: 1, 7: 2, 2: 3, 6: 4, 3: 5, 5: 6, 4: 7}
 GROUPS = ((0, 1), (1, 2), (3, 2), (5, 2), (7, 1))
 NN = (((1,), (0,)), ((), ()))
@@ -35,12 +35,13 @@
 
 def kernel(
     feats_hbm, routes_hbm, interp, w_value_hbm, w_attn_hbm, w_out_hbm, grad_out_hbm,
-    grad_feats, sums,
-    feats, routes, w_value, w_attn_t, w_out, grad_out, itp, v_rows,
-    ag, send_f, recv_f, send_r, recv_r, acc, rs_send, rs_recv,
-    con, con_rows, fet, fetched, attn_s, gm_s, ga_s, mixed_s, feats_t,
+    grad_feats, value_sums, other_sums,
+    column_feats, routes, w_value, w_attn_t, w_out, grad_out, itp, v_rows,
+    maps, send_f, recv_f, send_r, recv_r, acc, rs_send, rs_recv,
+    con, con_rows, fet, fetched, attn_s, gm_s, ga_s, mixed_s, w_value_t, value_s,
     pick_f, pick_r, mine_t, mine, route_s, gv_rows,
-    rp_send, rp_recv, rz_send, rz_recv, rx_recv, gz, gp,
+    value_plane, value_in, value_x, value_z, value_all,
+    other_plane, other_in, other_x, other_z, other_all,
     in_sem, itp_sem, ag_send_sem, ag_recv_sem, f_send_sem, f_recv_sem,
     r_send_sem, r_recv_sem, rs_send_sem, rs_recv_sem, sum_send_sem, sum_recv_sem,
 ):
@@ -95,7 +96,7 @@
     ins = [
         pltpu.make_async_copy(src, dst, in_sem.at[i])
         for i, (src, dst) in enumerate((
-            (feats_hbm, feats), (w_value_hbm, w_value), (routes_hbm, routes),
+            (feats_hbm.at[0], column_feats.at[0]), (w_value_hbm, w_value), (routes_hbm, routes),
             (w_attn_hbm, w_attn_t), (w_out_hbm, w_out), (grad_out_hbm, grad_out),
         ))
     ]
@@ -108,15 +109,19 @@
     for load in ins + loads:
         load.start()
 
+    def value_maps(q):
+        for l in range(2):
+            v_rows[l] = dot(w_value_t[...], column_feats[q, l * 128:(l + 1) * 128, :], NT)
+            for h in range(0, 8, 2):
+                for c in range(4):
+                    tiles = [v_rows[l, pl.ds((h + m) * 32 + c, 8, stride=4), :] for m in range(2)]
+                    rows = slice(l * 64 + h * 8, l * 64 + h * 8 + 16)
+                    maps[q, rows, c * 128:(c + 1) * 128] = jnp.concatenate(tiles, axis=0).astype(BF16)
+
     ins[0].wait()
     ins[1].wait()
-    values_t = dot(feats[0], w_value[...]).T
-    v_rows[0:256] = values_t[:, 0:128]
-    v_rows[256:512] = values_t[:, 128:256]
-    for k in range(0, 16, 2):
-        for c in range(4):
-            tiles = [v_rows[pl.ds((k + m) * 32 + c, 8, stride=4), :] for m in range(2)]
-            ag[0, k * 8:(k + 2) * 8, c * 128:(c + 1) * 128] = jnp.concatenate(tiles, axis=0).astype(BF16)
+    w_value_t[...] = w_value[...].astype(F32).T.astype(BF16)
+    value_maps(0)
     for load in ins[2:]:
         load.wait()
 
@@ -170,7 +175,7 @@
         pick_f[q] = piece.astype(BF16)
         pick_r[q] = piece.T.astype(BF16)
 
-    logits = dot(w_attn_t[...], feats[0], NT).reshape(H, 8, 256)
+    logits = dot(w_attn_t[...], column_feats[0], NT).reshape(H, 8, 256)
     powers = jnp.exp(logits - jnp.max(logits, axis=1, keepdims=True))
     attn_s[...] = (powers / jnp.sum(powers, axis=1, keepdims=True)).reshape(64, 256)
     gm_s[...] = dot(w_out[...], grad_out[0], NT)
@@ -197,7 +202,7 @@
     lax.fori_loop(0, 8, choose, 0)
 
     def answer(q):
-        send_f[q] = dot(pick_f[q], ag[q]).astype(BF16)
+        send_f[q] = dot(pick_f[q], maps[q]).astype(BF16)
     answer(0)
 
     pl.semaphore_wait(barrier, len(near))
@@ -207,9 +212,9 @@
             src, dst, to = (NZ - s) % NZ, NZ - 1 - s, right
         else:
             src, dst, to = s, s + 1, left
-        rows = pl.ds(half * 64, 64)
+        rows = pl.ds(half * 128, 128)
         return remote(
-            ag.at[PLACE[src], rows], ag.at[PLACE[dst], rows],
+            column_feats.at[PLACE[src], rows], column_feats.at[PLACE[dst], rows],
             ag_send_sem.at[side, s, half], ag_recv_sem.at[side, s, half], to, f,
         )
 
@@ -235,10 +240,9 @@
         for q in range(first, first + count):
             dst[q, block(p, 16), :] = src[q, block(p, 16), :]
 
-    for g in (4, 3, 2, 1, 0):
+    plane_send("f", send_f, recv_f, f_send_sem, f_recv_sem, 0)
+    for g in range(3):
         plane_send("r", send_r, recv_r, r_send_sem, r_recv_sem, g)
-    plane_send("f", send_f, recv_f, f_send_sem, f_recv_sem, 0)
-    feats_t[...] = feats[0].astype(F32).T.astype(BF16)
 
     def chain(side, s, half):
         rows = pl.ds(half * 64, 64)
@@ -248,10 +252,20 @@
             right if side == 0 else left, f,
         )
 
+    def lay_rows(total):
+        for k in range(16):
+            for c in range(4):
+                gv_rows[pl.ds(k * 32 + c, 8, stride=4), :] = total[k * 8:(k + 1) * 8, c * 128:(c + 1) * 128]
+
     def add_up(g):
         arrive(("r", g))
         for q in range(GROUPS[g][0], GROUPS[g][0] + GROUPS[g][1]):
-            acc[q] = dot(pick_r[q], recv_r[q])
+            total = dot(pick_r[q], recv_r[q])
+            acc[q] = total
+            lay_rows(total)
+            part = dot(gv_rows[0:256].astype(BF16), column_feats[q, 0:128, :])
+            part = part + dot(gv_rows[256:512].astype(BF16), column_feats[q, 128:256, :])
+            value_s[...] = part if q == 0 else value_s[...] + part
 
     def chain_send(side, s, half):
         rows = slice(half * 64, half * 64 + 64)
@@ -262,38 +276,81 @@
         rs_send[side, s, rows] = total.astype(BF16)
         send(("chain", side, s, half), chain(side, s, half))
 
-    add_up(4)
-    for side in range(2):
-        chain_send(side, 0, side)
+    def chain_step(s):
+        for order in range(2):
+            for side in range(2):
+                half = (1 - side + order) % 2
+                if s > 0 or half == side:
+                    chain_send(side, s, half)
+
     for s in range(1, 4):
         for side, _, half in ring_steps[s - 1]:
             arrive(("ring", side, s - 1, half))
             if (side, s, half) in ring_steps[s]:
                 send(("ring", side, s, half), ring(side, s, half))
         for q in range(GROUPS[s][0], GROUPS[s][0] + 2):
+            value_maps(q)
             answer(q)
         plane_send("f", send_f, recv_f, f_send_sem, f_recv_sem, s)
-        add_up(4 - s)
-        for order in range(2):
-            for side in range(2):
-                chain_send(side, s, (1 - side + order) % 2)
+        if s < 3:
+            plane_send("r", send_r, recv_r, r_send_sem, r_recv_sem, s + 2)
+        add_up(s - 1)
     for step in ring_steps[3]:
         arrive(("ring", *step))
+    value_maps(7)
     answer(7)
     plane_send("f", send_f, recv_f, f_send_sem, f_recv_sem, 4)
-    add_up(0)
-
-    total = acc[0]
-    for side in range(2):
-        for half in range(2):
-            arrive(("chain", side, 3, half))
-        total = total + rs_recv[side, 3].astype(F32)
-    for k in range(16):
-        for c in range(4):
-            gv_rows[pl.ds(k * 32 + c, 8, stride=4), :] = total[k * 8:(k + 1) * 8, c * 128:(c + 1) * 128]
-    grad_values = jnp.concatenate([gv_rows[0:256].T, gv_rows[256:512].T], axis=0).astype(BF16)
-    part_value = dot(feats_t[...], grad_values)
-    gm_value = dot(grad_values, w_value[...], NT)
+    add_up(4)
+    chain_step(0)
+    add_up(3)
+    part_value = value_s[...].T
+
+    def exchange(key, count, src, dst, here, device):
+        send_sem, recv_sem = sum_send_sem.at[key], sum_recv_sem.at[key]
+        copies = [remote(src(i), dst.at[here], send_sem, recv_sem, *device(i)) for i in range(1, count)]
+        send_many(key, copies, dst.at[pl.ds(0, count - 1)], send_sem, recv_sem)
+
+    def added(ref, count):
+        total = ref[0].astype(F32)
+        for q in range(1, count):
+            total = total + ref[q].astype(F32)
+        return total.astype(BF16)
+
+    stages = (
+        (value_plane, value_in, value_x, value_z, value_all),
+        (other_plane, other_in, other_x, other_z, other_all),
+    )
+
+    def share_out(n):
+        plane, inward = stages[n][0:2]
+        exchange(
+            n * 4, NP, lambda i: plane.at[lax.rem(p + i, NP)], inward, p, lambda i: (plane_tile(i), f)
+        )
+        inward[p] = plane[p]
+
+    def along_x(n):
+        arrive(n * 4)
+        across = stages[n][2]
+        across[f] = added(stages[n][1], NP)
+        exchange(n * 4 + 1, NX, lambda i: across.at[f], across, f, lambda i: (t, lax.rem(f + i, NX)))
+
+    def along_z(n):
+        arrive(n * 4 + 1)
+        up = stages[n][3]
+        up[z] = added(stages[n][2], NX)
+        exchange(n * 4 + 2, NZ, lambda i: up.at[z], up, z, lambda i: (column_tile(i), f))
+
+    def share_back(n):
+        arrive(n * 4 + 2)
+        back = stages[n][4]
+        back[p] = added(stages[n][3], NZ)
+        exchange(n * 4 + 3, NP, lambda i: back.at[p], back, p, lambda i: (plane_tile(i), f))
+
+    for q in range(NP):
+        lanes = slice((q // 4) * 128, (q // 4 + 1) * 128)
+        k = q % 4
+        value_plane[q] = part_value[k * 64:(k + 1) * 64, lanes].astype(BF16)
+    share_out(0)
 
     for g in range(4):
         arrive(("f", g))
@@ -305,117 +362,99 @@
     lax.fori_loop(0, 4, fetch, 0)
     arrive(("f", 4))
 
-    def sample(h, _):
-        grad_mixed = gm_s[block(h, 32), :]
-        weights = attn_s[block(h, 8), :]
-        maps = fetched[block(h, 64), :] + dot(mine[block(h, 64), 896:1024], recv_f[7])
-        for i in range(8):
+    def sample(e, _):
+        rows = fetched[block(e, 128), :] + dot(mine[block(e, 128), 896:1024], recv_f[7])
+        for i in range(16):
             for c in range(4):
-                fet[pl.ds(i * 32 + c, 8, stride=4), :] = maps[i * 8:(i + 1) * 8, c * 128:(c + 1) * 128]
-        mixed = jnp.zeros((32, 256), F32)
-        grads = []
-        for i in range(8):
-            sampled = dot(fet[i * 32:(i + 1) * 32, :].astype(BF16), itp[h * 8 + i], NT)
-            mixed = mixed + weights[i:i + 1] * sampled
-            grads.append(jnp.sum(grad_mixed * sampled, axis=0, keepdims=True))
-        mixed_s[block(h, 32), :] = mixed.astype(BF16)
-        ga_s[block(h, 8), :] = jnp.concatenate(grads, axis=0)
+                fet[pl.ds(i * 32 + c, 8, stride=4), :] = rows[i * 8:(i + 1) * 8, c * 128:(c + 1) * 128]
+        for m in range(2):
+            h = e * 2 + m
+            grad_mixed = gm_s[block(h, 32), :]
+            weights = attn_s[block(h, 8), :]
+            mixed = jnp.zeros((32, 256), F32)
+            grads = []
+            for i in range(8):
+                k = m * 8 + i
+                sampled = dot(fet[k * 32:(k + 1) * 32, :].astype(BF16), itp[h * 8 + i], NT)
+                mixed = mixed + weights[i:i + 1] * sampled
+                grads.append(jnp.sum(grad_mixed * sampled, axis=0, keepdims=True))
+            mixed_s[block(h, 32), :] = mixed.astype(BF16)
+            ga_s[block(h, 8), :] = jnp.concatenate(grads, axis=0)
         return 0
-    lax.fori_loop(0, H, sample, 0)
+    lax.fori_loop(0, 2, sample, 0)
+    along_x(0)
+    chain_step(1)
+    lax.fori_loop(2, 4, sample, 0)
 
     attn = attn_s[...].reshape(H, 8, 256)
     grad_attn = ga_s[...].reshape(H, 8, 256)
     inner = jnp.sum(attn * grad_attn, axis=1, keepdims=True)
     grad_logits = (attn * (grad_attn - inner)).reshape(64, 256)
-    part_attn = dot(grad_logits.astype(BF16), feats[0])
+    part_attn = dot(grad_logits.astype(BF16), column_feats[0])
     part_out = dot(mixed_s[...], grad_out[0])
 
     for q in range(NP):
         lanes = slice((q // 4) * 128, (q // 4 + 1) * 128)
         k = q % 4
-        rp_send[q, 0:64] = part_value[k * 64:(k + 1) * 64, lanes].astype(BF16)
-        rp_send[q, 64:128] = part_out[k * 64:(k + 1) * 64, lanes].astype(BF16)
-        rp_send[q, 128:144] = part_attn[k * 16:(k + 1) * 16, lanes].astype(BF16)
-
-    def exchange(stage, count, src, dst, device):
-        send_sem, recv_sem = sum_send_sem.at[stage], sum_recv_sem.at[stage]
-        copies = [remote(src(i), dst[1], send_sem, recv_sem, *device(i)) for i in range(1, count)]
-        send_many(stage, copies, dst[0].at[pl.ds(0, count - 1)], send_sem, recv_sem)
-
-    exchange(
-        0, NP, lambda i: rp_send.at[lax.rem(p + i, NP)], (rp_recv, rp_recv.at[p]), lambda i: (plane_tile(i), f)
-    )
-    rp_recv[p] = rp_send[p]
+        other_plane[q, 0:64] = part_out[k * 64:(k + 1) * 64, lanes].astype(BF16)
+        other_plane[q, 64:80] = part_attn[k * 16:(k + 1) * 16, lanes].astype(BF16)
+    share_out(1)
+    along_z(0)
     grad_query = dot(grad_logits.T.astype(BF16), w_attn_t[...])
-    grad_feats[0] = (grad_query + gm_value).astype(BF16)
-    arrive(0)
-    total = rp_recv[0].astype(F32)
-    for q in range(1, NP):
-        total = total + rp_recv[q].astype(F32)
-    for q in range(NZ):
-        rows = [total[q * 8:(q + 1) * 8], total[64 + q * 8:64 + (q + 1) * 8], total[128:144]]
-        rz_send[q] = jnp.concatenate(rows, axis=0).astype(BF16)
-    exchange(
-        1, NZ, lambda i: rz_send.at[lax.rem(z + i, NZ)], (rz_recv, rz_recv.at[z]), lambda i: (column_tile(i), f)
-    )
-    rz_recv[z] = rz_send[z]
-    arrive(1)
-    total = rz_recv[0].astype(F32)
-    for q in range(1, NZ):
-        total = total + rz_recv[q].astype(F32)
-    rx_recv[f] = total.astype(BF16)
-    exchange(
-        2, NX, lambda i: rx_recv.at[f], (rx_recv, rx_recv.at[f]), lambda i: (t, lax.rem(f + i, NX))
-    )
-    arrive(2)
-    total = rx_recv[0].astype(F32)
-    for q in range(1, NX):
-        total = total + rx_recv[q].astype(F32)
-    gz[z] = total[0:16].astype(BF16)
-    exchange(3, NZ, lambda i: gz.at[z], (gz, gz.at[z]), lambda i: (column_tile(i), f))
+    along_x(1)
+    chain_step(2)
+    along_z(1)
+    share_back(0)
+    chain_step(3)
+    share_back(1)
+    own = acc[0]
+    for side in range(2):
+        for half in range(2):
+            arrive(("chain", side, 3, half))
+        own = own + rs_recv[side, 3].astype(F32)
+    lay_rows(own)
+    grad_values = jnp.concatenate([gv_rows[0:256].T, gv_rows[256:512].T], axis=0).astype(BF16)
+    grad_feats[0] = (grad_query + dot(grad_values, w_value_t[...])).astype(BF16)
     arrive(3)
-    gathered = [gz[q].astype(F32) for q in range(NZ)]
-    gp[p] = jnp.concatenate(
-        [g[0:8] for g in gathered] + [g[8:16] for g in gathered] + [total[16:32]], axis=0
-    ).astype(BF16)
-    exchange(4, NP, lambda i: gp.at[p], (gp, gp.at[p]), lambda i: (plane_tile(i), f))
-    arrive(4)
-    sums[...] = gp[...]
+    value_sums[...] = value_all[...]
+    arrive(7)
+    other_sums[...] = other_all[...]
 
     settle()
 
 
-def finish(grad_in, sums, grad_feats, grad_w_value, grad_w_attn_t, grad_w_out):
+def finish(grad_in, value_sums, other_sums, grad_feats, grad_w_value, grad_w_attn_t, grad_w_out):
     factor = 1.0 / math.sqrt(NX * NZ * NP * 256)
     grad_feats[...] = grad_in[...]
     for q in range(NP):
         lanes = slice((q // 4) * 128, (q // 4 + 1) * 128)
         k = q % 4
-        grad_w_value[k * 64:(k + 1) * 64, lanes] = sums[q, 0:64].astype(F32) * factor
-        grad_w_out[k * 64:(k + 1) * 64, lanes] = sums[q, 64:128].astype(F32) * factor
-        grad_w_attn_t[k * 16:(k + 1) * 16, lanes] = sums[q, 128:144].astype(F32) * factor
+        grad_w_value[k * 64:(k + 1) * 64, lanes] = value_sums[q].astype(F32) * factor
+        grad_w_out[k * 64:(k + 1) * 64, lanes] = other_sums[q, 0:64].astype(F32) * factor
+        grad_w_attn_t[k * 16:(k + 1) * 16, lanes] = other_sums[q, 64:80].astype(F32) * factor
 
 
 def per_device(feats, routes, interp, w_value, w_attn, w_out, grad_out):
     vmem = pl.BlockSpec(memory_space=pltpu.VMEM)
     dma = pltpu.SemaphoreType.DMA
-    moved, sums = pl.pallas_call(
+    moved, value_sums, other_sums = pl.pallas_call(
         kernel,
         out_shape=(
             jax.ShapeDtypeStruct((1, 256, 256), BF16),
-            jax.ShapeDtypeStruct((NP, SHARE, 128), BF16),
+            jax.ShapeDtypeStruct((NP, SHARES[0], 128), BF16),
+            jax.ShapeDtypeStruct((NP, SHARES[1], 128), BF16),
         ),
         in_specs=[pl.BlockSpec(memory_space=pltpu.HBM)] * 7,
-        out_specs=(vmem,) * 2,
+        out_specs=(vmem,) * 3,
         scratch_shapes=[
-            pltpu.VMEM((1, 256, 256), BF16),
+            pltpu.VMEM((8, 256, 256), BF16),
             pltpu.VMEM((1, 64, 64), jnp.int32),
             pltpu.VMEM((256, 256), BF16),
             pltpu.VMEM((64, 256), BF16),
             pltpu.VMEM((256, 256), BF16),
             pltpu.VMEM((1, 256, 256), BF16),
             pltpu.VMEM((64, 256, 128), BF16),
-            pltpu.VMEM((512, 128), F32),
+            pltpu.VMEM((2, 256, 128), F32),
             pltpu.VMEM((8, 128, 512), BF16),
             pltpu.VMEM((8, 128, 512), BF16),
             pltpu.VMEM((8, 128, 512), BF16),
@@ -426,26 +465,25 @@
             pltpu.VMEM((2, 4, 128, 512), BF16),
             pltpu.VMEM((256, 128), F32),
             pltpu.VMEM((512, 512), BF16),
-            pltpu.VMEM((256, 128), F32),
+            pltpu.VMEM((512, 128), F32),
             pltpu.VMEM((512, 512), F32),
             pltpu.VMEM((64, 256), F32),
             pltpu.VMEM((256, 256), F32),
             pltpu.VMEM((64, 256), F32),
             pltpu.VMEM((256, 256), BF16),
             pltpu.VMEM((256, 256), BF16),
+            pltpu.VMEM((256, 256), F32),
             pltpu.VMEM((8, 128, 128), BF16),
             pltpu.VMEM((8, 128, 128), BF16),
             pltpu.VMEM((8, 128, 512), BF16),
             pltpu.VMEM((512, 1024), BF16),
             pltpu.VMEM((8, 128), jnp.int32),
             pltpu.VMEM((512, 128), F32),
-            pltpu.VMEM((NP, SHARE, 128), BF16),
-            pltpu.VMEM((NP, SHARE, 128), BF16),
-            pltpu.VMEM((NZ, 32, 128), BF16),
-            pltpu.VMEM((NZ, 32, 128), BF16),
-            pltpu.VMEM((NX, 32, 128), BF16),
-            pltpu.VMEM((NZ, 16, 128), BF16),
-            pltpu.VMEM((NP, SHARE, 128), BF16),
+            *[
+                pltpu.VMEM((count, rows, 128), BF16)
+                for rows in SHARES
+                for count in (NP, NP, NX, NZ, NP)
+            ],
             dma((6,)),
             dma((H,)),
             dma((2, 4, 2)),
@@ -456,8 +494,8 @@
             dma((5,)),
             dma((2, 4, 2)),
             dma((2, 4, 2)),
-            dma((5,)),
-            dma((5,)),
+            dma((8,)),
+            dma((8,)),
         ],
         compiler_params=pltpu.CompilerParams(
             collective_id=0, has_side_effects=True, vmem_limit_bytes=63 * 1024 * 1024
@@ -471,9 +509,9 @@
             jax.ShapeDtypeStruct((64, 256), F32),
             jax.ShapeDtypeStruct((256, 256), F32),
         ),
-        in_specs=[vmem] * 2,
+        in_specs=[vmem] * 3,
         out_specs=(vmem,) * 4,
-    )(moved, sums)
+    )(moved, value_sums, other_sums)
     return grads[0], grads[1], grads[2].T, grads[3]
 
 

time: 72.6 us -> 67.5 us (0.930)
  Pallas kernels: 71.9 us -> 66.7 us
    pallas_call x1, Pallas kernels: 70 us -> 64.8 us  [per_device(): pl.pallas_call(kernel, out_shape=(jax.ShapeDtypeStruct((1, 256, 256), BF1...]
where the time goes in v3:
time: 67.5 us; the launch traced here: 67.4 us
  Pallas kernels  66.7 us (99%)
    pallas_call x1, Pallas kernels, per_device(): pl.pallas_call(kernel, out_shape=(jax.ShapeDtypeStruct((1, 256, 256), BF1...  64.8 us
    pallas_call x1, Pallas kernels, per_device(): pl.pallas_call(finish, out_shape=(jax.ShapeDtypeStruct((1, 256, 256), BF1...  1.92 us

profile of v3, /device:TPU:1, one launch (start us, length us, event | category | flops | bytes accessed | tf_op | source)
XLA Modules:
  0.0 67.4 jit_solution(1790777870157493916)
XLA Ops:
  0.6 64.8 %shard_map.102 = (bf16[1,256,256]{2,1,0:T(8,128)(2,1)}, bf16[8,64,128]{2,1,0:T(8,128)(2,1)}, bf16[8,80,128]{2,1,0:T(8,128)(2,1)}) custom-call(bf16[1,256,256]{2,1,0:T(8,128)(2,1)} %feats_hbm.1, s32[1,64,64]{2,1,0:T(8,128)} %routes_hbm.1, bf16[1,64,256,128]{3,2,1,0:T(8,128)(2,1)} %interp.1, bf16[256,256]{1,0:T(8,128)(2,1)} %w_value_hbm.1, ...), custom_call_target="tpu_custom_call" | custom-call | tf_op jit(solution)/shard_map/pallas_call | solution.py:440
  65.5 1.9 %shard_map.103 = (bf16[1,256,256]{2,1,0:T(8,128)(2,1)}, f32[256,256]{1,0:T(8,128)}, f32[64,256]{1,0:T(8,128)}, f32[256,256]{1,0:T(8,128)}) custom-call(bf16[1,256,256]{2,1,0:T(8,128)(2,1)} %get-tuple-element.11.grad_in, bf16[8,64,128]{2,1,0:T(8,128)(2,1)} %get-tuple-element.12.value_sums, bf16[8,80,128]{2,1,0:T(8,128)(2,1)} %get-tuple-element.13.other_sums), custom_call_target="tpu_custom_call" | custom-call | tf_op jit(solution)/shard_map/pallas_call | solution.py:504

commit v4 on v3

--- a/solution.py
+++ b/solution.py
@@ -36,7 +36,7 @@
 def kernel(
     feats_hbm, routes_hbm, interp, w_value_hbm, w_attn_hbm, w_out_hbm, grad_out_hbm,
     grad_feats, value_sums, other_sums,
-    column_feats, routes, w_value, w_attn_t, w_out, grad_out, itp, v_rows,
+    column_feats, routes, w_value, w_attn_t, w_out, grad_out, itp, itp_t, v_rows,
     maps, send_f, recv_f, send_r, recv_r, acc, rs_send, rs_recv,
     con, con_rows, fet, fetched, attn_s, gm_s, ga_s, mixed_s, w_value_t, value_s,
     pick_f, pick_r, mine_t, mine, route_s, gv_rows,
@@ -118,11 +118,7 @@
                     rows = slice(l * 64 + h * 8, l * 64 + h * 8 + 16)
                     maps[q, rows, c * 128:(c + 1) * 128] = jnp.concatenate(tiles, axis=0).astype(BF16)
 
-    ins[0].wait()
-    ins[1].wait()
-    w_value_t[...] = w_value[...].astype(F32).T.astype(BF16)
-    value_maps(0)
-    for load in ins[2:]:
+    for load in ins:
         load.wait()
 
     route_s[...] = jnp.full(route_s.shape, -1, jnp.int32)
@@ -156,24 +152,9 @@
 
     mine_now = picks(jnp.broadcast_to(route_s[pl.ds(p, 1), :], (128, 128)), owner_z + row_plane)
     mine_wide = dot(mine_now.astype(BF16), eighth((128, 512)))
-    mine_wide_t = dot(mine_now.T[0:64].astype(BF16), eighth((128, 1024)))
-    readers = jnp.broadcast_to(
-        jnp.broadcast_to(route_s[...][:, None, :], (8, 2, 128)).reshape(16, 128)[None], (8, 16, 128)
-    ).reshape(128, 128)
-    asked = picks(readers, owner_z + p)
-    piece_of = lax.rem(lax.div(row, 4), 2) * 8 + lax.div(row, 8)
-    to_piece = dot(asked.astype(BF16), one_hot(piece_of == lax.div(lane, 8)))
-    keep = same_row((128, 128))
     keep_wide = same_row((128, 512))
-    keep_long = same_row((512, 128))
     for q in range(8):
         mine_t[q] = jnp.where(keep_wide, by_eight(mine_wide[q * 16:(q + 1) * 16]), 0.0).astype(BF16)
-        mine[:, q * 128:(q + 1) * 128] = jnp.where(
-            keep_long, by_eight(mine_wide_t[:, q * 128:(q + 1) * 128]), 0.0
-        ).astype(BF16)
-        piece = jnp.where(keep, by_eight(to_piece[q * 16:(q + 1) * 16]), 0.0)
-        pick_f[q] = piece.astype(BF16)
-        pick_r[q] = piece.T.astype(BF16)
 
     logits = dot(w_attn_t[...], column_feats[0], NT).reshape(H, 8, 256)
     powers = jnp.exp(logits - jnp.max(logits, axis=1, keepdims=True))
@@ -203,8 +184,6 @@
 
     def answer(q):
         send_f[q] = dot(pick_f[q], maps[q]).astype(BF16)
-    answer(0)
-
     pl.semaphore_wait(barrier, len(near))
 
     def ring(side, s, half):
@@ -240,9 +219,29 @@
         for q in range(first, first + count):
             dst[q, block(p, 16), :] = src[q, block(p, 16), :]
 
+    for g in range(5):
+        plane_send("r", send_r, recv_r, r_send_sem, r_recv_sem, g)
+
+    w_value_t[...] = w_value[...].astype(F32).T.astype(BF16)
+    value_maps(0)
+    mine_wide_t = dot(mine_now.T[0:64].astype(BF16), eighth((128, 1024)))
+    readers = jnp.broadcast_to(
+        jnp.broadcast_to(route_s[...][:, None, :], (8, 2, 128)).reshape(16, 128)[None], (8, 16, 128)
+    ).reshape(128, 128)
+    asked = picks(readers, owner_z + p)
+    piece_of = lax.rem(lax.div(row, 4), 2) * 8 + lax.div(row, 8)
+    to_piece = dot(asked.astype(BF16), one_hot(piece_of == lax.div(lane, 8)))
+    keep = same_row((128, 128))
+    keep_long = same_row((512, 128))
+    for q in range(8):
+        mine[:, q * 128:(q + 1) * 128] = jnp.where(
+            keep_long, by_eight(mine_wide_t[:, q * 128:(q + 1) * 128]), 0.0
+        ).astype(BF16)
+        piece = jnp.where(keep, by_eight(to_piece[q * 16:(q + 1) * 16]), 0.0)
+        pick_f[q] = piece.astype(BF16)
+        pick_r[q] = piece.T.astype(BF16)
+    answer(0)
     plane_send("f", send_f, recv_f, f_send_sem, f_recv_sem, 0)
-    for g in range(3):
-        plane_send("r", send_r, recv_r, r_send_sem, r_recv_sem, g)
 
     def chain(side, s, half):
         rows = pl.ds(half * 64, 64)
@@ -283,6 +282,10 @@
                 if s > 0 or half == side:
                     chain_send(side, s, half)
 
+    def turn(j, _):
+        itp_t[j] = itp[j].T
+        return 0
+
     for s in range(1, 4):
         for side, _, half in ring_steps[s - 1]:
             arrive(("ring", side, s - 1, half))
@@ -292,9 +295,8 @@
             value_maps(q)
             answer(q)
         plane_send("f", send_f, recv_f, f_send_sem, f_recv_sem, s)
-        if s < 3:
-            plane_send("r", send_r, recv_r, r_send_sem, r_recv_sem, s + 2)
         add_up(s - 1)
+        lax.fori_loop((s - 1) * 22, min(s * 22, 64), turn, 0)
     for step in ring_steps[3]:
         arrive(("ring", *step))
     value_maps(7)
@@ -375,7 +377,7 @@
             grads = []
             for i in range(8):
                 k = m * 8 + i
-                sampled = dot(fet[k * 32:(k + 1) * 32, :].astype(BF16), itp[h * 8 + i], NT)
+                sampled = dot(fet[k * 32:(k + 1) * 32, :].astype(BF16), itp_t[h * 8 + i])
                 mixed = mixed + weights[i:i + 1] * sampled
                 grads.append(jnp.sum(grad_mixed * sampled, axis=0, keepdims=True))
             mixed_s[block(h, 32), :] = mixed.astype(BF16)
@@ -454,6 +456,7 @@
             pltpu.VMEM((256, 256), BF16),
             pltpu.VMEM((1, 256, 256), BF16),
             pltpu.VMEM((64, 256, 128), BF16),
+            pltpu.VMEM((64, 128, 256), BF16),
             pltpu.VMEM((2, 256, 128), F32),
             pltpu.VMEM((8, 128, 512), BF16),
             pltpu.VMEM((8, 128, 512), BF16),

time: 67.5 us -> 66 us (0.978)
  Pallas kernels: 66.7 us -> 65.3 us
    pallas_call x1, Pallas kernels: 64.8 us -> 63.3 us  [per_device(): pl.pallas_call(kernel, out_shape=(jax.ShapeDtypeStruct((1, 256, 256), BF1...]
where the time goes in v4:
time: 66 us; the launch traced here: 65.9 us
  Pallas kernels  65.3 us (99%)
    pallas_call x1, Pallas kernels, per_device(): pl.pallas_call(kernel, out_shape=(jax.ShapeDtypeStruct((1, 256, 256), BF1...  63.3 us
    pallas_call x1, Pallas kernels, per_device(): pl.pallas_call(finish, out_shape=(jax.ShapeDtypeStruct((1, 256, 256), BF1...  1.92 us

profile of v4, /device:TPU:1, one launch (start us, length us, event | category | flops | bytes accessed | tf_op | source)
XLA Modules:
  0.0 65.9 jit_solution(2958074318231158549)
XLA Ops:
  0.6 63.3 %shard_map.102 = (bf16[1,256,256]{2,1,0:T(8,128)(2,1)}, bf16[8,64,128]{2,1,0:T(8,128)(2,1)}, bf16[8,80,128]{2,1,0:T(8,128)(2,1)}) custom-call(bf16[1,256,256]{2,1,0:T(8,128)(2,1)} %feats_hbm.1, s32[1,64,64]{2,1,0:T(8,128)} %routes_hbm.1, bf16[1,64,256,128]{3,2,1,0:T(8,128)(2,1)} %interp.1, bf16[256,256]{1,0:T(8,128)(2,1)} %w_value_hbm.1, ...), custom_call_target="tpu_custom_call" | custom-call | tf_op jit(solution)/shard_map/pallas_call | solution.py:442
  64.0 1.9 %shard_map.103 = (bf16[1,256,256]{2,1,0:T(8,128)(2,1)}, f32[256,256]{1,0:T(8,128)}, f32[64,256]{1,0:T(8,128)}, f32[256,256]{1,0:T(8,128)}) custom-call(bf16[1,256,256]{2,1,0:T(8,128)(2,1)} %get-tuple-element.11.grad_in, bf16[8,64,128]{2,1,0:T(8,128)(2,1)} %get-tuple-element.12.value_sums, bf16[8,80,128]{2,1,0:T(8,128)(2,1)} %get-tuple-element.13.other_sums), custom_call_target="tpu_custom_call" | custom-call | tf_op jit(solution)/shard_map/pallas_call | solution.py:507

commit v5 on v4

--- a/solution.py
+++ b/solution.py
@@ -42,7 +42,7 @@
     pick_f, pick_r, mine_t, mine, route_s, gv_rows,
     value_plane, value_in, value_x, value_z, value_all,
     other_plane, other_in, other_x, other_z, other_all,
-    in_sem, itp_sem, ag_send_sem, ag_recv_sem, f_send_sem, f_recv_sem,
+    moved, in_sem, out_sem, itp_sem, ag_send_sem, ag_recv_sem, f_send_sem, f_recv_sem,
     r_send_sem, r_recv_sem, rs_send_sem, rs_recv_sem, sum_send_sem, sum_recv_sem,
 ):
     t = lax.axis_index("tile")
@@ -416,11 +416,20 @@
         own = own + rs_recv[side, 3].astype(F32)
     lay_rows(own)
     grad_values = jnp.concatenate([gv_rows[0:256].T, gv_rows[256:512].T], axis=0).astype(BF16)
-    grad_feats[0] = (grad_query + dot(grad_values, w_value_t[...])).astype(BF16)
+    moved[...] = (grad_query + dot(grad_values, w_value_t[...])).astype(BF16)
+    outs = [
+        pltpu.make_async_copy(src, dst, out_sem.at[i])
+        for i, (src, dst) in enumerate((
+            (moved, grad_feats.at[0]), (value_all, value_sums), (other_all, other_sums),
+        ))
+    ]
+    outs[0].start()
     arrive(3)
-    value_sums[...] = value_all[...]
+    outs[1].start()
     arrive(7)
-    other_sums[...] = other_all[...]
+    outs[2].start()
+    for out in outs:
+        out.wait()
 
     settle()
 
@@ -447,7 +456,7 @@
             jax.ShapeDtypeStruct((NP, SHARES[1], 128), BF16),
         ),
         in_specs=[pl.BlockSpec(memory_space=pltpu.HBM)] * 7,
-        out_specs=(vmem,) * 3,
+        out_specs=(pl.BlockSpec(memory_space=pl.ANY),) * 3,
         scratch_shapes=[
             pltpu.VMEM((8, 256, 256), BF16),
             pltpu.VMEM((1, 64, 64), jnp.int32),
@@ -487,7 +496,9 @@
                 for rows in SHARES
                 for count in (NP, NP, NX, NZ, NP)
             ],
+            pltpu.VMEM((256, 256), BF16),
             dma((6,)),
+            dma((3,)),
             dma((H,)),
             dma((2, 4, 2)),
             dma((2, 4, 2)),

time: 66 us -> 66 us (level)
  no operation moved by 1% of the time
where the time goes in v5:
time: 66 us; the launch traced here: 65.8 us
  Pallas kernels  65.2 us (99%)
    pallas_call x1, Pallas kernels, per_device(): pl.pallas_call(kernel, out_shape=(jax.ShapeDtypeStruct((1, 256, 256), BF1...  63.3 us
    pallas_call x1, Pallas kernels, per_device(): pl.pallas_call(finish, out_shape=(jax.ShapeDtypeStruct((1, 256, 256), BF1...  1.92 us

profile of v5, /device:TPU:1, one launch (start us, length us, event | category | flops | bytes accessed | tf_op | source)
XLA Modules:
  0.0 65.8 jit_solution(9645315121394597477)
XLA Ops:
  0.6 63.3 %shard_map.102 = (bf16[1,256,256]{2,1,0:T(8,128)(2,1)}, bf16[8,64,128]{2,1,0:T(8,128)(2,1)}, bf16[8,80,128]{2,1,0:T(8,128)(2,1)}) custom-call(bf16[1,256,256]{2,1,0:T(8,128)(2,1)} %feats_hbm.1, s32[1,64,64]{2,1,0:T(8,128)} %routes_hbm.1, bf16[1,64,256,128]{3,2,1,0:T(8,128)(2,1)} %interp.1, bf16[256,256]{1,0:T(8,128)(2,1)} %w_value_hbm.1, ...), custom_call_target="tpu_custom_call" | custom-call | tf_op jit(solution)/shard_map/pallas_call | solution.py:451
  63.9 1.9 %shard_map.103 = (bf16[1,256,256]{2,1,0:T(8,128)(2,1)}, f32[256,256]{1,0:T(8,128)}, f32[64,256]{1,0:T(8,128)}, f32[256,256]{1,0:T(8,128)}) custom-call(bf16[1,256,256]{2,1,0:T(8,128)(2,1)} %get-tuple-element.11.grad_in, bf16[8,64,128]{2,1,0:T(8,128)(2,1)} %get-tuple-element.12.value_sums, bf16[8,80,128]{2,1,0:T(8,128)(2,1)} %get-tuple-element.13.other_sums), custom_call_target="tpu_custom_call" | custom-call | tf_op jit(solution)/shard_map/pallas_call | solution.py:518
